TPU v7x, 32 devices: a whole 2x2x4 slice. The times are simulated.
32 devices in a mesh: dp: 2 (over x), expert: 16 (over z, y, core).
Axes of the slice: x: 2, y: 2, z: 4, core: 2. Of those that a mesh axis runs over, the one named last changes fastest.
Arguments:
- tokens: bfloat16 [2, 1024, 2048], P(None, 'expert', 'dp'), may hold values from -6 to 6
- cotangent: bfloat16 [2, 1024, 2048], P(None, 'expert', 'dp'), may hold values from -6 to 6
- routes: int32 [2, 1024, 2], P(None, 'expert'), may hold values from 0 to 15, all different within a row; in each aligned block of 64 rows (0 to 63, 64 to 127, ..., all dimensions but the last counted through in order) at most 12 rows name the same one
- gates: float32 [2, 1024, 2], P(None, 'expert'), may hold values from 0.25 to 1
- source: int32 [16], replicated, may hold values from 0 to 15, as said below
- w_gate_up: bfloat16 [16, 2048, 2, 1024], P('expert', None, None, 'dp'), may hold values from -0.125 to 0.125
- w_down: bfloat16 [16, 1024, 2048], P('expert', 'dp'), may hold values from -0.1875 to 0.1875
- moment_first: bfloat16 [16, 1024, 2048], P('expert', 'dp'), may hold values from -6 to 6
- moment_second: bfloat16 [16, 1024, 2048], P('expert', 'dp'), may hold values from 0.25 to 4
Outputs:
- layer_out: bfloat16 [2, 1024, 2048], P(None, 'expert', 'dp')
- token_grad: bfloat16 [2, 1024, 2048], P(None, 'expert', 'dp')
- update_dir: bfloat16 [16, 1024, 2048], P('expert', 'dp')
- new_first: bfloat16 [16, 1024, 2048], P('expert', 'dp')
- new_second: bfloat16 [16, 1024, 2048], P('expert', 'dp')
Inputs may be any that keep to these rules, and one draw needn't show every extreme that they name: `routes`: in each micro-batch, the 64 tokens of one index of expert name no expert more than 12 times, a bound that some block reaches. source[source[s]] = s for every slot; 8 slots take another slot's expert.
All inputs are finite; a program needn't handle non-finite values.
Results may differ from a plain program's by a relative error of at most 0.018.
Values may be sent and summed in bfloat16 or wider, within the bound.
No kernel may reach another device: no remote copies, remote signals or barrier semaphores. Data moves between devices by JAX's collectives and lax.ppermute only.
A program may use at most 128 MiB of HBM per device.

v0:
```python
import jax
import jax.numpy as jnp
from jax import lax
from jax.sharding import PartitionSpec as P

contract_first = (((0,), (0,)), ((), ()))
contract_second = (((1,), (1,)), ((), ()))


def split_back(flattened, templates):
    outputs = []
    offset = 0
    for template in templates:
        element_count = template.size
        outputs.append(flattened[offset : offset + element_count].reshape(template.shape))
        offset = offset + element_count
    return outputs


def relocate_state(arrays, source, experts):
    flattened = jnp.concatenate([member.reshape(-1) for member in arrays]).reshape(experts, -1)
    spread = lax.all_to_all(flattened, "expert", split_axis=0, concat_axis=0, tiled=True)
    picked = jnp.take(spread, source, axis=0)
    final = lax.all_to_all(picked, "expert", split_axis=0, concat_axis=0, tiled=True)
    return split_back(final.reshape(-1), arrays)


def per_device(
    tokens, cotangent, routes, gates, source, w_gate_up, w_down, moment_first, moment_second
):
    experts = lax.axis_size("expert")
    micro_count, token_count, part_width = tokens.shape
    model_width = w_gate_up.shape[1]
    hidden_part = w_gate_up.shape[3]
    top_count = routes.shape[2]
    capacity = max(2, 3 * token_count * top_count // (2 * experts))
    slots = experts * capacity
    column_ids = jnp.arange(experts, dtype=jnp.int32)
    w_gate_up, w_down, moment_first, moment_second = relocate_state(
        (w_gate_up, w_down, moment_first, moment_second), source, experts
    )
    target = jnp.sum(jnp.where(routes[..., None] == column_ids, source, 0), axis=-1)
    slot_ids = jnp.arange(slots, dtype=jnp.int32)
    picks_list = []
    plain_list = []
    slot_gate_list = []
    for micro in range(micro_count):
        chosen = target[micro].reshape(-1)
        onehot = (chosen[:, None] == column_ids).astype(jnp.int32)
        position = jnp.sum((jnp.cumsum(onehot, axis=0) - onehot) * onehot, axis=1)
        slot_of = (chosen * capacity + position).reshape(token_count, top_count)
        picks = []
        slot_gate = jnp.zeros((slots,), jnp.float32)
        for choice_k in range(top_count):
            match = slot_of[:, choice_k][:, None] == slot_ids
            picks.append(match.astype(jnp.bfloat16))
            slot_gate = slot_gate + jnp.sum(
                jnp.where(match, gates[micro][:, choice_k : choice_k + 1], 0.0), axis=0
            )
        plain = picks[0]
        choice_k = 1
        plain = plain + picks[choice_k]
        picks_list.append(picks)
        plain_list.append(plain)
        slot_gate_list.append(slot_gate)
    gate_up_flat = w_gate_up.reshape(model_width, 2 * hidden_part)
    down_local = w_down.reshape(hidden_part, model_width)
    source_tokens, source_grads = (
        lax.all_gather(tokens, "dp", axis=2, tiled=True),
        lax.all_gather(cotangent, "dp", axis=2, tiled=True),
    )
    down_grad = jnp.zeros((hidden_part, model_width), jnp.float32)
    layer_parts = []
    grad_parts = []
    for micro in range(micro_count):
        plain = plain_list[micro]
        picks = picks_list[micro]
        slot_gate = slot_gate_list[micro]
        row_tokens = lax.dot_general(
            plain, source_tokens[micro], contract_first, preferred_element_type=jnp.float32
        ).astype(jnp.bfloat16)
        row_grads = (
            lax.dot_general(
                plain, source_grads[micro], contract_first, preferred_element_type=jnp.float32
            )
            * slot_gate[:, None]
        ).astype(jnp.bfloat16)
        send_width = row_tokens.shape[1]
        arrived_tokens, arrived_grads = (
            lax.all_to_all(
                row_tokens.reshape(experts, capacity, send_width),
                "expert",
                split_axis=0,
                concat_axis=0,
                tiled=True,
            ),
            lax.all_to_all(
                row_grads.reshape(experts, capacity, send_width),
                "expert",
                split_axis=0,
                concat_axis=0,
                tiled=True,
            ),
        )
        expert_in = arrived_tokens.reshape(slots, model_width)
        grad_in = arrived_grads.reshape(slots, model_width)
        both = jnp.dot(expert_in, gate_up_flat, preferred_element_type=jnp.float32).reshape(
            slots, 2, hidden_part
        )
        gate_pre = both[:, 0]
        up_pre = both[:, 1]
        gate_sig = jax.nn.sigmoid(gate_pre)
        hidden = (gate_pre * gate_sig * up_pre).astype(jnp.bfloat16)
        partial_out = jnp.dot(hidden, down_local, preferred_element_type=jnp.float32)
        summed_out = lax.psum_scatter(
            partial_out.reshape(experts, capacity, model_width).astype(jnp.bfloat16),
            "dp",
            scatter_dimension=2,
            tiled=True,
        )
        returned_out = lax.all_to_all(summed_out, "expert", split_axis=0, concat_axis=0, tiled=True)
        returned_out = returned_out.reshape(slots, -1)
        combined = jnp.zeros((token_count, returned_out.shape[1]), jnp.float32)
        for choice_k in range(top_count):
            combined = combined + gates[micro][:, choice_k : choice_k + 1] * jnp.dot(
                picks[choice_k], returned_out, preferred_element_type=jnp.float32
            )
        layer_parts.append(combined.astype(jnp.bfloat16))
        hidden_grad = lax.dot_general(
            grad_in, down_local, contract_second, preferred_element_type=jnp.float32
        )
        down_grad = down_grad + lax.dot_general(
            hidden, grad_in, contract_first, preferred_element_type=jnp.float32
        )
        gate_grad = hidden_grad * up_pre * gate_sig * (1.0 + gate_pre * (1.0 - gate_sig))
        up_grad = hidden_grad * gate_pre * gate_sig
        both_grad = (
            jnp.stack([gate_grad, up_grad], axis=1)
            .astype(jnp.bfloat16)
            .reshape(slots, 2 * hidden_part)
        )
        partial_in = lax.dot_general(
            both_grad, gate_up_flat, contract_second, preferred_element_type=jnp.float32
        )
        summed_in = lax.psum_scatter(
            partial_in.reshape(experts, capacity, model_width).astype(jnp.bfloat16),
            "dp",
            scatter_dimension=2,
            tiled=True,
        )
        returned_in = lax.all_to_all(summed_in, "expert", split_axis=0, concat_axis=0, tiled=True)
        returned_in = returned_in.reshape(slots, -1)
        gathered = jnp.zeros((token_count, returned_in.shape[1]), jnp.float32)
        for choice_k in range(top_count):
            gathered = gathered + jnp.dot(
                picks[choice_k], returned_in, preferred_element_type=jnp.float32
            )
        grad_parts.append(gathered.astype(jnp.bfloat16))
    first = (
        0.9 * moment_first.reshape(hidden_part, model_width).astype(jnp.float32) + 0.1 * down_grad
    )
    second = (
        0.999 * moment_second.reshape(hidden_part, model_width).astype(jnp.float32)
        + 0.001 * down_grad * down_grad
    )
    update = first / (jnp.sqrt(second) + 1e-08)
    results = (
        update.astype(jnp.bfloat16).reshape(moment_first.shape),
        first.astype(jnp.bfloat16).reshape(moment_first.shape),
        second.astype(jnp.bfloat16).reshape(moment_first.shape),
    )
    return (jnp.stack(layer_parts), jnp.stack(grad_parts), results[0], results[1], results[2])


def solution(mesh):
    placed = (
        P(None, "expert", "dp"),
        P(None, "expert", "dp"),
        P(None, "expert", None),
        P(None, "expert", None),
        P(),
        P("expert", None, None, "dp"),
        P("expert", "dp", None),
        P("expert", "dp", None),
        P("expert", "dp", None),
    )
    return jax.shard_map(
        per_device,
        mesh=mesh,
        in_specs=placed,
        out_specs=(
            P(None, "expert", "dp"),
            P(None, "expert", "dp"),
            P("expert", "dp", None),
            P("expert", "dp", None),
            P("expert", "dp", None),
        ),
        check_vma=False,
    )
```

profile of v0, /device:TPU:8, one launch (start us, length us, event | category | flops | bytes accessed | tf_op | source)
XLA Modules:
  0.0 1075.1 jit_solution(2853437736110352333)
XLA Ops:
  7.2 2.4 copy.98
  10.8 1.1 copy-done
  11.9 4.3 copy.95
  16.2 91.1 %pad_maximum_fusion = bf16[5242880]{0:T(1024)(128)(2,1)} fusion(bf16[1048576]{0:T(1024)(128)(2,1)S(1)} %bitcast.199, bf16[1048576]{0:T(1024)(128)(2,1)S(1)} %bitcast.200, bf16[1048576]{0:T(1024)(128)(2,1)S(1)} %bitcast.201, bf16[2097152]{0:T(1024)(128)(2,1)S(1)} %bitcast.198), kind=kLoop, calls=%fused_computation.3 | loop fusion | flops 41943040 | bytes 20971520 | tf_op jit(solution)/shard_map/concatenate | solution.py:21
  107.3 16.0 %all_to_all.48 = bf16[16,1,327680]{2,1,0:T(2,128)(2,1)} reshape(bf16[5242880]{0:T(1024)(128)(2,1)} %pad_maximum_fusion) | data formatting | bytes 20971520 | tf_op jit(solution)/shard_map/all_to_all | solution.py:22
  123.8 65.3 %reduce.2 = bf16[16,327680]{1,0:T(8,128)(2,1)} reduce(bf16[16,1,327680]{2,1,0:T(2,128)(2,1)} %all_to_all.48, bf16[]{:T(256)} %broadcast.103), dimensions={1}, to_apply=%all_to_all.48.reduce_sub_computation | reduce | bytes 20971522 | tf_op jit(solution)/shard_map/all_to_all | solution.py:22
  189.1 19.5 %reshape.215 = bf16[16,2,163840]{2,1,0:T(2,128)(2,1)} reshape(bf16[16,327680]{1,0:T(8,128)(2,1)} %reduce.2) | data formatting | bytes 20971520
  208.7 6.4 all-to-all-start.1
  217.0 9.0 all_gather.6
  227.3 1.1 reshape.168
  228.5 212.2 %all-to-all-done.1 = bf16[16,2,163840]{2,1,0:T(2,128)(2,1)} async-done(((bf16[16,2,163840]{2,1,0:T(2,128)(2,1)}), bf16[16,2,163840]{2,1,0:T(2,128)(2,1)}, u32[]{:S(2)}, u32[]{:S(2)}) %all-to-all-start.1) | async-done | bytes 10485792 | tf_op jit(solution)/shard_map/all_to_all | solution.py:22
  440.7 6.6 all-to-all-start.4
  447.3 18.4 %reshape.216 = bf16[16,1,327680]{2,1,0:T(2,128)(2,1)} reshape(bf16[16,2,163840]{2,1,0:T(2,128)(2,1)} %all-to-all-done.1) | data formatting | bytes 20971520
  465.7 18.9 %copy.108 = bf16[16,1,327680]{2,0,1:T(8,128)(2,1)S(1)} copy(bf16[16,1,327680]{2,1,0:T(2,128)(2,1)} %reshape.216) | data formatting | bytes 20971520
  484.5 2.0 mini-gather-slice.5
  486.5 2.2 fusion.104
  488.8 9.8 gather_fusion.2
  498.6 10.2 gather_fusion.1
  508.8 4.6 gather_fusion
  513.4 12.7 %fusion = bf16[16,1,327680]{2,0,1:T(8,128)(2,1)} fusion(bf16[16,109056]{1,0:T(8,128)(2,1)} %gather_fusion.2, bf16[16,109312]{1,0:T(8,128)(2,1)} %gather_fusion.1, bf16[16,109312]{1,0:T(8,128)(2,1)} %gather_fusion, pred[16]{0:T(512)(128)(4,1)S(1)} %compare_and_fusion), kind=kLoop, calls=%fused_computation.5 | loop fusion | flops 36700160 | bytes 20971536 | tf_op jit(solution)/shard_map/jit(_take)/select_n | solution.py:23
  526.1 13.2 %reduce.3 = bf16[16,327680]{1,0:T(8,128)(2,1)} reduce(bf16[16,1,327680]{2,0,1:T(8,128)(2,1)} %fusion, bf16[]{:T(256)} %broadcast.103), dimensions={1}, to_apply=%copy.80.reduce_sub_computation | reduce | bytes 20971522 | tf_op jit(solution)/shard_map/jit(_take)/select_n | solution.py:23
  539.3 19.7 %reshape.217 = bf16[16,2,163840]{2,1,0:T(2,128)(2,1)} reshape(bf16[16,327680]{1,0:T(8,128)(2,1)} %reduce.3) | data formatting | bytes 20971520
  559.1 6.2 all-to-all-start.2
  565.8 9.0 all_gather.7
  576.1 1.1 reshape.174
  577.2 1.3 reshape.209
  578.5 212.3 %all-to-all-done.2 = bf16[16,2,163840]{2,1,0:T(2,128)(2,1)} async-done(((bf16[16,2,163840]{2,1,0:T(2,128)(2,1)}), bf16[16,2,163840]{2,1,0:T(2,128)(2,1)}, u32[]{:S(2)}, u32[]{:S(2)}) %all-to-all-start.2) | async-done | bytes 10485792 | tf_op jit(solution)/shard_map/all_to_all | solution.py:24
  790.9 6.6 all-to-all-start.8
  797.5 18.4 %reshape.218 = bf16[16,1,327680]{2,1,0:T(2,128)(2,1)} reshape(bf16[16,2,163840]{2,1,0:T(2,128)(2,1)} %all-to-all-done.2) | data formatting | bytes 20971520
  815.9 64.7 %reduce = bf16[16,327680]{1,0:T(8,128)(2,1)} reduce(bf16[16,1,327680]{2,1,0:T(2,128)(2,1)} %reshape.218, bf16[]{:T(256)} %constant.43), dimensions={1}, to_apply=%all_to_all.40.reduce_sub_computation | reduce | bytes 20971522 | tf_op jit(solution)/shard_map/all_to_all | solution.py:24
  880.5 14.4 %slice.100 = bf16[2560,2048]{1,0:T(8,128)(2,1)} reshape(bf16[16,327680]{1,0:T(8,128)(2,1)} %reduce) | data formatting | bytes 20971520 | tf_op jit(solution)/shard_map/slice | solution.py:15
  894.9 14.3 %slice.96 = bf16[5120,1024]{1,0:T(8,128)(2,1)} reshape(bf16[16,327680]{1,0:T(8,128)(2,1)} %reduce) | data formatting | bytes 20971520 | tf_op jit(solution)/shard_map/slice | solution.py:15
  909.2 4.6 slice_bitcast_fusion
  913.8 6.9 copy.81
  920.7 3.7 fusion.115
  926.5 3.2 convolution_convert_fusion
  930.2 1.1 reshape.161
  931.3 6.0 all-to-all-start
  937.4 1.0 reshape.175
  938.5 2.8 fusion.67
  942.0 4.7 fusion.11
  947.4 1.1 reshape.171
  948.6 13.0 %all-to-all-done = bf16[16,12,2048]{2,1,0:T(8,128)(2,1)S(1)} async-done(((bf16[16,12,2048]{2,1,0:T(8,128)(2,1)}), bf16[16,12,2048]{2,1,0:T(8,128)(2,1)S(1)}, u32[]{:S(2)}, u32[]{:S(2)}) %all-to-all-start) | async-done | bytes 786464 | tf_op jit(solution)/shard_map/all_to_all | solution.py:90
  961.6 5.6 all-to-all-start.6
  967.2 1.1 reshape.207
  968.3 4.0 fusion.114
  972.6 3.1 convolution_convert_fusion.2
  975.7 2.0 copy.87
  977.7 13.6 %all-to-all-done.6 = bf16[16,12,2048]{2,1,0:T(8,128)(2,1)S(1)} async-done(((bf16[16,12,2048]{2,1,0:T(8,128)(2,1)}), bf16[16,12,2048]{2,1,0:T(8,128)(2,1)S(1)}, u32[]{:S(2)}, u32[]{:S(2)}) %all-to-all-start.6) | async-done | bytes 786464 | tf_op jit(solution)/shard_map/all_to_all | solution.py:97
  991.4 5.6 all-to-all-start.5
  997.2 2.5 fusion.66
  1000.4 2.0 copy.93
  1002.4 8.2 all-to-all-done.5
  1010.6 4.9 all-to-all-start.9
  1015.8 4.7 fusion.8
  1020.5 2.9 fusion.60
  1023.3 2.0 copy.83
  1025.3 3.9 all-to-all-done.9
  1029.2 4.9 all-to-all-start.3
  1034.1 8.2 fusion.18
  1042.4 2.0 copy.90
  1045.1 2.6 all-to-all-done.3
  1047.8 4.9 all-to-all-start.7
  1053.8 12.5 %all-to-all-done.7 = bf16[16,12,1024]{2,1,0:T(8,128)(2,1)S(1)} async-done(((bf16[16,12,1024]{2,1,0:T(8,128)(2,1)}), bf16[16,12,1024]{2,1,0:T(8,128)(2,1)S(1)}, u32[]{:S(2)}, u32[]{:S(2)}) %all-to-all-start.7) | async-done | bytes 393248 | tf_op jit(solution)/shard_map/all_to_all | solution.py:151
  (127 shorter events, 15.9 us)
Async XLA Ops:
  7.2 2.4 copy-start.7
  7.2 3.0 copy-start.8
  9.6 2.3 copy-start
  208.6 6.4 copy-start.21
  208.6 6.4 copy-start.23
  208.6 8.4 copy-start.11
  208.7 232.1 %all-to-all-start.1 = ((bf16[16,2,163840]{2,1,0:T(2,128)(2,1)}), bf16[16,2,163840]{2,1,0:T(2,128)(2,1)}, u32[]{:S(2)}, u32[]{:S(2)}) async-start(bf16[16,2,163840]{2,1,0:T(2,128)(2,1)} %reshape.215), calls=%async_computation.1 | async-start | bytes 20971520 | tf_op jit(solution)/shard_map/all_to_all | solution.py:22
  226.1 0.8 copy-start.3
  440.7 118.3 %all-to-all-start.4 = ((bf16[16,12,2048]{2,1,0:T(8,128)(2,1)}), bf16[16,12,2048]{2,1,0:T(8,128)(2,1)}, u32[]{:S(2)}, u32[]{:S(2)}) async-start(bf16[16,12,2048]{2,1,0:T(8,128)(2,1)} %reshape.168), calls=%async_computation.5 | async-start | bytes 2097152 | tf_op jit(solution)/shard_map/all_to_all | solution.py:90
  559.0 6.2 copy-start.22
  559.0 6.7 copy-start.12
  559.1 231.8 %all-to-all-start.2 = ((bf16[16,2,163840]{2,1,0:T(2,128)(2,1)}), bf16[16,2,163840]{2,1,0:T(2,128)(2,1)}, u32[]{:S(2)}, u32[]{:S(2)}) async-start(bf16[16,2,163840]{2,1,0:T(2,128)(2,1)} %reshape.217), calls=%async_computation.2 | async-start | bytes 20971520 | tf_op jit(solution)/shard_map/all_to_all | solution.py:24
  565.2 0.5 copy-start.13
  565.3 0.5 copy-start.15
  574.8 0.8 copy-start.9
  790.9 140.5 %all-to-all-start.8 = ((bf16[16,12,2048]{2,1,0:T(8,128)(2,1)}), bf16[16,12,2048]{2,1,0:T(8,128)(2,1)S(1)}, u32[]{:S(2)}, u32[]{:S(2)}) async-start(bf16[16,12,2048]{2,1,0:T(8,128)(2,1)} %reshape.174), calls=%async_computation.11 | async-start | bytes 2097152 | tf_op jit(solution)/shard_map/all_to_all | solution.py:97
  797.4 178.3 %reduce-scatter.7.cloned.1.call-start = ((), (), s32[]{:S(2)}) async-start(), calls=%async_computation.15 | async-start | bytes 1179648 | tf_op jit(solution)/shard_map/reduce_scatter | solution.py:115
  924.5 14.0 %copy-start.1 = (f32[192,2,512]{2,0,1:T(8,128)}, f32[192,2,512]{2,0,1:T(8,128)S(1)}, u32[]{:S(2)}) copy-start(f32[192,2,512]{2,0,1:T(8,128)S(1)} %fusion.115) | copy-start | bytes 2359300
  924.5 5.2 copy-start.4
  931.3 30.2 %all-to-all-start = ((bf16[16,12,2048]{2,1,0:T(8,128)(2,1)}), bf16[16,12,2048]{2,1,0:T(8,128)(2,1)S(1)}, u32[]{:S(2)}, u32[]{:S(2)}) async-start(bf16[16,12,2048]{2,1,0:T(8,128)(2,1)} %reshape.161), calls=%async_computation | async-start | bytes 2097152 | tf_op jit(solution)/shard_map/all_to_all | solution.py:90
  937.4 63.1 %reduce-scatter.11.cloned.1.call-start = ((), (), s32[]{:S(2)}) async-start(), calls=%async_computation.17 | async-start | bytes 1179648 | tf_op jit(solution)/shard_map/reduce_scatter | solution.py:145
  937.4 9.3 copy-start.19
  937.4 9.4 copy-start.17
  942.0 5.0 copy-start.10
  961.6 29.8 %all-to-all-start.6 = ((bf16[16,12,2048]{2,1,0:T(8,128)(2,1)}), bf16[16,12,2048]{2,1,0:T(8,128)(2,1)S(1)}, u32[]{:S(2)}, u32[]{:S(2)}) async-start(bf16[16,12,2048]{2,1,0:T(8,128)(2,1)} %reshape.171), calls=%async_computation.8 | async-start | bytes 2097152 | tf_op jit(solution)/shard_map/all_to_all | solution.py:97
  967.2 56.2 %reduce-scatter.5.cloned.1.call-start = ((), (), s32[]{:S(2)}) async-start(), calls=%async_computation.14 | async-start | bytes 1179648 | tf_op jit(solution)/shard_map/reduce_scatter | solution.py:115
  991.4 19.2 %all-to-all-start.5 = ((bf16[16,12,1024]{2,1,0:T(8,128)(2,1)}), bf16[16,12,1024]{2,1,0:T(8,128)(2,1)S(1)}, u32[]{:S(2)}, u32[]{:S(2)}) async-start(bf16[16,12,1024]{2,1,0:T(8,128)(2,1)} %copy.87), calls=%async_computation.7 | async-start | bytes 1048576 | tf_op jit(solution)/shard_map/all_to_all | solution.py:121
  1010.6 9.8 copy-start.5
  1010.6 18.6 %all-to-all-start.9 = ((bf16[16,12,1024]{2,1,0:T(8,128)(2,1)}), bf16[16,12,1024]{2,1,0:T(8,128)(2,1)S(1)}, u32[]{:S(2)}, u32[]{:S(2)}) async-start(bf16[16,12,1024]{2,1,0:T(8,128)(2,1)} %copy.93), calls=%async_computation.13 | async-start | bytes 1048576 | tf_op jit(solution)/shard_map/all_to_all | solution.py:151
  1015.6 26.9 %reduce-scatter.9.cloned.1.call-start = ((), (), s32[]{:S(2)}) async-start(), calls=%async_computation.16 | async-start | bytes 1179648 | tf_op jit(solution)/shard_map/reduce_scatter | solution.py:145
  1020.5 13.7 %copy-start.2 = (f32[192,2,512]{2,0,1:T(8,128)S(1)}, f32[192,2,512]{2,0,1:T(8,128)}, u32[]{:S(2)}) copy-start(f32[192,2,512]{2,0,1:T(8,128)} %copy-done.1) | copy-start | bytes 2359300
  1029.2 18.6 %all-to-all-start.3 = ((bf16[16,12,1024]{2,1,0:T(8,128)(2,1)}), bf16[16,12,1024]{2,1,0:T(8,128)(2,1)S(1)}, u32[]{:S(2)}, u32[]{:S(2)}) async-start(bf16[16,12,1024]{2,1,0:T(8,128)(2,1)} %copy.83), calls=%async_computation.4 | async-start | bytes 1048576 | tf_op jit(solution)/shard_map/all_to_all | solution.py:121
  1034.1 10.3 copy-start.6
  1042.4 10.4 copy-start.16
  1042.4 10.7 copy-start.14
  1042.4 10.9 %copy-start.20 = (f32[64]{0:T(128)S(1)}, f32[64]{0:T(128)}, u32[]{:S(2)}) copy-start(f32[64]{0:T(128)} %copy-done.19) | copy-start | bytes 772
  1042.4 11.2 %copy-start.18 = (f32[64]{0:T(128)S(1)}, f32[64]{0:T(128)}, u32[]{:S(2)}) copy-start(f32[64]{0:T(128)} %copy-done.17) | copy-start | bytes 772
  1047.8 18.6 %all-to-all-start.7 = ((bf16[16,12,1024]{2,1,0:T(8,128)(2,1)}), bf16[16,12,1024]{2,1,0:T(8,128)(2,1)S(1)}, u32[]{:S(2)}, u32[]{:S(2)}) async-start(bf16[16,12,1024]{2,1,0:T(8,128)(2,1)} %copy.90), calls=%async_computation.10 | async-start | bytes 1048576 | tf_op jit(solution)/shard_map/all_to_all | solution.py:151
Sparse Core Ops, SparseCore 0:
  929.8 18.3 reduce-scatter.6
  950.5 17.4 reduce-scatter.10
  975.8 18.3 reduce-scatter.4
  1020.6 18.3 reduce-scatter.8
where the time goes:
time: 1090 us; the launch traced here: 1080 us
  waiting for transfers between devices  479 us (44%)
  other arithmetic  250 us (23%)
  local copies, waits for them, and re-layouts  212 us (19%)
  starting transfers between devices  58 us (5%)
  matrix products  43.4 us (4%)
  blocking collectives  18.1 us (2%)
  between operations  14.6 us (1%)
    all_to_all x1, waiting for transfers between devices, relocate_state(): lax.all_to_all(picked, 'expert', split_axis=0, concat_axis=0, tiled=True)  212 us
    all_to_all x1, waiting for transfers between devices, relocate_state(): lax.all_to_all(flattened, 'expert', split_axis=0, concat_axis=0, tiled=True)  212 us
    unnamed x57, local copies, waits for them, and re-layouts  106 us
    concatenate x1, other arithmetic, relocate_state(): jnp.concatenate([member.reshape(-1) for member in arrays])  91.1 us
    all_to_all x1, other arithmetic, relocate_state(): lax.all_to_all(flattened, 'expert', split_axis=0, concat_axis=0, tiled=True)  65.3 us
    all_to_all x1, other arithmetic, relocate_state(): lax.all_to_all(picked, 'expert', split_axis=0, concat_axis=0, tiled=True)  64.7 us
    gather x5, local copies, waits for them, and re-layouts, relocate_state(): picked = jnp.take(spread, source, axis=0)  28.9 us
    slice x2, local copies, waits for them, and re-layouts, split_back(): flattened[offset:offset + element_count].reshape(template.shape)  28.7 us
  transfers between devices with their start and end apart: 14, of which 8 were waited for; matrix products, arithmetic and copies ran while one was open for 28% of the time, Pallas kernels for 0%

commit v1 on v0

v1 whole, which is shorter than its diff:
```python
import jax
import jax.numpy as jnp
from jax import lax
from jax.experimental import pallas as pl
from jax.experimental.pallas import tpu as pltpu
from jax.sharding import PartitionSpec as P

contract_first = (((0,), (0,)), ((), ()))
contract_second = (((1,), (1,)), ((), ()))


def exchange(blocks):
    return lax.all_to_all(blocks, "expert", split_axis=0, concat_axis=0, tiled=True)


def copy_block(order_ref, block_ref, out_ref):
    out_ref[...] = block_ref[...]


def reorder(blocks, order):
    count, rows, width = blocks.shape
    return pl.pallas_call(
        copy_block,
        out_shape=jax.ShapeDtypeStruct(blocks.shape, blocks.dtype),
        grid_spec=pltpu.PrefetchScalarGridSpec(
            num_scalar_prefetch=1,
            grid=(count,),
            in_specs=[pl.BlockSpec((1, rows, width), lambda s, order_ref: (order_ref[s], 0, 0))],
            out_specs=pl.BlockSpec((1, rows, width), lambda s, order_ref: (s, 0, 0)),
        ),
        name="reorder",
    )(order, blocks)


def gather_features(rows):
    parts = lax.axis_size("dp")
    if parts == 2:
        other = lax.ppermute(rows, "dp", ((0, 1), (1, 0)))
        first = lax.axis_index("dp") == 0
        return [jnp.where(first, rows, other), jnp.where(first, other, rows)]
    whole = lax.all_gather(rows, "dp", axis=0, tiled=False)
    return [whole[part] for part in range(parts)]


def scatter_sum(partial):
    parts = lax.axis_size("dp")
    if parts == 2:
        half = partial.shape[1] // 2
        low, high = partial[:, :half], partial[:, half:]
        first = lax.axis_index("dp") == 0
        keep, send = jnp.where(first, low, high), jnp.where(first, high, low)
        other = lax.ppermute(send, "dp", ((0, 1), (1, 0)))
        return (keep.astype(jnp.float32) + other.astype(jnp.float32)).astype(jnp.bfloat16)
    return lax.psum_scatter(partial, "dp", scatter_dimension=1, tiled=True)


def relocate(array, source, experts):
    blocks = array.reshape(experts, array.shape[1] // experts, array.shape[2])
    return exchange(reorder(exchange(blocks), source)).reshape(array.shape[1:])


def per_device(
    tokens, cotangent, routes, gates, source, w_gate_up, w_down, moment_first, moment_second
):
    experts = lax.axis_size("expert")
    micro_count, token_count, part_width = tokens.shape
    model_width = w_gate_up.shape[1]
    hidden_part = w_gate_up.shape[3]
    top_count = routes.shape[2]
    capacity = max(2, 3 * token_count * top_count // (2 * experts))
    per_expert = micro_count * capacity
    slots = experts * per_expert
    all_tokens = micro_count * token_count

    pairs = token_count * top_count
    chosen = routes.reshape(micro_count, pairs)
    same = chosen[:, :, None] == chosen[:, None, :]
    order = jnp.arange(pairs, dtype=jnp.int32)
    earlier = order[None, :] < order[:, None]
    position = jnp.sum((same & earlier).astype(jnp.int32), axis=2)
    micro_ids = jnp.arange(micro_count, dtype=jnp.int32)[:, None]
    place = (chosen * per_expert + micro_ids * capacity + position).reshape(all_tokens, top_count)
    slot_ids = jnp.arange(slots, dtype=jnp.int32)
    flat_gates = gates.reshape(all_tokens, top_count)
    matches = [place[:, k][:, None] == slot_ids for k in range(top_count)]
    picks = [match.astype(jnp.bfloat16) for match in matches]
    plain = sum(picks[1:], picks[0])
    slot_gate = sum(
        jnp.sum(jnp.where(matches[k], flat_gates[:, k : k + 1], 0.0), axis=0)
        for k in range(top_count)
    )

    row_tokens = lax.dot_general(
        plain,
        tokens.reshape(all_tokens, part_width),
        contract_first,
        preferred_element_type=jnp.float32,
    ).astype(jnp.bfloat16)
    row_grads = (
        lax.dot_general(
            plain,
            cotangent.reshape(all_tokens, part_width),
            contract_first,
            preferred_element_type=jnp.float32,
        )
        * slot_gate[:, None]
    ).astype(jnp.bfloat16)
    grad_blocks = row_grads.reshape(experts, per_expert, part_width)
    here_tokens = exchange(row_tokens.reshape(experts, per_expert, part_width))
    here_grads = exchange(grad_blocks)
    token_parts = gather_features(here_tokens.reshape(slots, part_width))
    grad_parts = gather_features(here_grads.reshape(slots, part_width))

    gate_up = w_gate_up.reshape(model_width, 2 * hidden_part)
    down = w_down.reshape(hidden_part, model_width)

    expert_in = jnp.concatenate(token_parts, axis=1)
    grad_in = jnp.concatenate(grad_parts, axis=1)
    both = jnp.dot(expert_in, gate_up, preferred_element_type=jnp.float32).reshape(
        slots, 2, hidden_part
    )
    gate_pre = both[:, 0]
    up_pre = both[:, 1]
    gate_sig = jax.nn.sigmoid(gate_pre)
    hidden = (gate_pre * gate_sig * up_pre).astype(jnp.bfloat16)
    partial_out = jnp.dot(hidden, down, preferred_element_type=jnp.float32).astype(jnp.bfloat16)
    summed_out = scatter_sum(partial_out)
    back = exchange(
        jnp.concatenate([summed_out, hidden], axis=1).reshape(experts, per_expert, -1)
    )
    back_out = back[:, :, :part_width].reshape(slots, part_width)
    back_hidden = back[:, :, part_width:]
    layer_out = sum(
        flat_gates[:, k : k + 1] * jnp.dot(picks[k], back_out, preferred_element_type=jnp.float32)
        for k in range(top_count)
    )

    there = exchange(reorder(jnp.concatenate([back_hidden, grad_blocks], axis=2), source))
    there = there.reshape(slots, hidden_part + part_width)
    there_hidden = there[:, :hidden_part]
    there_grads = jnp.concatenate(gather_features(there[:, hidden_part:]), axis=1)

    hidden_grad = lax.dot_general(
        grad_in, down, contract_second, preferred_element_type=jnp.float32
    )
    gate_grad = hidden_grad * up_pre * gate_sig * (1.0 + gate_pre * (1.0 - gate_sig))
    up_grad = hidden_grad * gate_pre * gate_sig
    both_grad = (
        jnp.stack([gate_grad, up_grad], axis=1)
        .astype(jnp.bfloat16)
        .reshape(slots, 2 * hidden_part)
    )
    partial_in = lax.dot_general(
        both_grad, gate_up, contract_second, preferred_element_type=jnp.float32
    ).astype(jnp.bfloat16)
    summed_in = scatter_sum(partial_in)
    back_in = exchange(summed_in.reshape(experts, per_expert, part_width))
    token_grad = jnp.dot(
        plain, back_in.reshape(slots, part_width), preferred_element_type=jnp.float32
    )

    old_first = relocate(moment_first, source, experts)
    old_second = relocate(moment_second, source, experts)
    down_grad = lax.dot_general(
        there_hidden, there_grads, contract_first, preferred_element_type=jnp.float32
    )
    first = 0.9 * old_first.astype(jnp.float32) + 0.1 * down_grad
    second = 0.999 * old_second.astype(jnp.float32) + 0.001 * down_grad * down_grad
    update = first / (jnp.sqrt(second) + 1e-08)
    shape = moment_first.shape
    return (
        layer_out.astype(jnp.bfloat16).reshape(tokens.shape),
        token_grad.astype(jnp.bfloat16).reshape(tokens.shape),
        update.astype(jnp.bfloat16).reshape(shape),
        first.astype(jnp.bfloat16).reshape(shape),
        second.astype(jnp.bfloat16).reshape(shape),
    )


def solution(mesh):
    placed = (
        P(None, "expert", "dp"),
        P(None, "expert", "dp"),
        P(None, "expert", None),
        P(None, "expert", None),
        P(),
        P("expert", None, None, "dp"),
        P("expert", "dp", None),
        P("expert", "dp", None),
        P("expert", "dp", None),
    )
    return jax.shard_map(
        per_device,
        mesh=mesh,
        in_specs=placed,
        out_specs=(
            P(None, "expert", "dp"),
            P(None, "expert", "dp"),
            P("expert", "dp", None),
            P("expert", "dp", None),
            P("expert", "dp", None),
        ),
        check_vma=False,
    )
```

time: 1090 us -> 375 us (0.34)
  waiting for transfers between devices: 479 us -> 162 us
  other arithmetic: 250 us -> 12.9 us
  local copies, waits for them, and re-layouts: 212 us -> 17.9 us
  blocking collectives: 18.1 us -> 77.2 us
  Pallas kernels: 0 us -> 30.1 us
  matrix products: 43.4 us -> 23.4 us
  between operations: 14.6 us -> 0.89 us
    all_to_all x10 -> x7, waiting for transfers between devices: 478 us -> 114 us  [exchange(): lax.all_to_all(blocks, 'expert', split_axis=0, concat_axis=0, tiled=True)]
    all_to_all x2 -> x0, other arithmetic: 130 us -> none  [the longest x1 65.3 us: relocate_state(): lax.all_to_all(flattened, 'expert', split_axis=0, concat_axis=0, tiled=True)]
    unnamed x57 -> x19, local copies, waits for them, and re-layouts: 106 us -> 6.29 us
    concatenate x1 -> x2, other arithmetic: 91.1 us -> 2.18 us  [the longest x1 1.09 us: per_device(): jnp.concatenate([summed_out, hidden], axis=1)]
    all_to_all x0 -> x2, blocking collectives: none -> 77.2 us  [exchange(): lax.all_to_all(blocks, 'expert', split_axis=0, concat_axis=0, tiled=True)]
    ppermute x0 -> x5, waiting for transfers between devices: none -> 47.2 us  [the longest x2 31.9 us: scatter_sum(): other = lax.ppermute(send, 'dp', ((0, 1), (1, 0)))]
    pallas_call x0 -> x3, Pallas kernels: none -> 30.1 us  [reorder(): pl.pallas_call(copy_block, out_shape=jax.ShapeDtypeStruct(blocks.shape, b...]
    gather x5 -> x0, local copies, waits for them, and re-layouts: 28.9 us -> none  [relocate_state(): picked = jnp.take(spread, source, axis=0)]
  transfers between devices with their start and end apart: 14 -> 12, of which waited for: 8 -> 10; matrix products, arithmetic and copies ran while one was open for 28% -> 11% of each run, Pallas kernels for 0% -> 8%
where the time goes in v1:
time: 375 us; the launch traced here: 371 us
  waiting for transfers between devices  162 us (43%)
  blocking collectives  77.2 us (21%)
  starting transfers between devices  47.1 us (13%)
  Pallas kernels  30.1 us (8%)
  matrix products  23.4 us (6%)
  local copies, waits for them, and re-layouts  17.9 us (5%)
  other arithmetic  12.9 us (3%)
    all_to_all x7, waiting for transfers between devices, exchange(): lax.all_to_all(blocks, 'expert', split_axis=0, concat_axis=0, tiled=True)  114 us
    all_to_all x2, blocking collectives, exchange(): lax.all_to_all(blocks, 'expert', split_axis=0, concat_axis=0, tiled=True)  77.2 us
    all_to_all x7, starting transfers between devices, exchange(): lax.all_to_all(blocks, 'expert', split_axis=0, concat_axis=0, tiled=True)  40.4 us
    ppermute x2, waiting for transfers between devices, scatter_sum(): other = lax.ppermute(send, 'dp', ((0, 1), (1, 0)))  31.9 us
    pallas_call x3, Pallas kernels, reorder(): pl.pallas_call(copy_block, out_shape=jax.ShapeDtypeStruct(blocks.shape, b...  30.1 us
    ppermute x3, waiting for transfers between devices, gather_features(): other = lax.ppermute(rows, 'dp', ((0, 1), (1, 0)))  15.3 us
  transfers between devices with their start and end apart: 12, of which 10 were waited for; matrix products, arithmetic and copies ran while one was open for 11% of the time, Pallas kernels for 8%

profile of v1, /device:TPU:8, one launch (start us, length us, event | category | flops | bytes accessed | tf_op | source)
XLA Modules:
  0.0 370.9 jit_solution(16327827523220233408)
XLA Ops:
  0.7 0.9 copy.23
  1.6 0.7 broadcast_multiply_fusion
  2.3 0.1 eq.52
  2.5 0.2 convert_reduce_fusion
  2.6 0.1 reduce_sum.30
  2.9 0.1 mul.113
  3.0 0.1 add.58
  3.1 2.3 convolution_convert_fusion.2
  5.4 6.3 %all-to-all-start = ((bf16[16,24,1024]{2,1,0:T(8,128)(2,1)}), bf16[16,24,1024]{2,1,0:T(8,128)(2,1)}, u32[]{:S(2)}, u32[]{:S(2)}) async-start(bf16[16,24,1024]{2,1,0:T(8,128)(2,1)} %bitcast.4), calls=%async_computation | async-start | bytes 1572864 | tf_op jit(solution)/shard_map/all_to_all | solution.py:13
  11.7 0.1 reshape.124
  11.8 0.1 select_reduce_fusion
  12.0 0.5 multiply_convert_fusion
  12.5 18.3 %all-to-all-done = bf16[16,24,1024]{2,1,0:T(8,128)(2,1)} async-done(((bf16[16,24,1024]{2,1,0:T(8,128)(2,1)}), bf16[16,24,1024]{2,1,0:T(8,128)(2,1)}, u32[]{:S(2)}, u32[]{:S(2)}) %all-to-all-start) | async-done | bytes 786464 | tf_op jit(solution)/shard_map/all_to_all | solution.py:13
  30.8 24.8 %all_to_all.45 = bf16[16,24,1024]{2,1,0:T(8,128)(2,1)} all-to-all(bf16[16,24,1024]{2,1,0:T(8,128)(2,1)S(1)} %bitcast.127), channel_id=1, replica_groups=mesh['dp'=2,'expert'=16] {'expert'}, dimensions={0} | all-to-all | bytes 1572864 | tf_op jit(solution)/shard_map/all_to_all | solution.py:13
  55.5 52.4 %all_to_all.46.block_ref = bf16[16,32,2048]{2,1,0:T(8,128)(2,1)} all-to-all(bf16[16,32,2048]{2,1,0:T(8,128)(2,1)} %bitcast.139), channel_id=1, replica_groups=mesh['dp'=2,'expert'=16] {'expert'}, dimensions={0} | all-to-all | bytes 4194304 | tf_op jit(solution)/shard_map/all_to_all | solution.py:13
  107.9 5.0 %all-to-all-start.4 = ((bf16[16,32,2048]{2,1,0:T(8,128)(2,1)}), bf16[16,32,2048]{2,1,0:T(8,128)(2,1)}, u32[]{:S(2)}, u32[]{:S(2)}) async-start(bf16[16,32,2048]{2,1,0:T(8,128)(2,1)} %bitcast.140), calls=%async_computation.4 | async-start | bytes 4194304 | tf_op jit(solution)/shard_map/all_to_all | solution.py:13
  113.0 1.5 collective-permute-start
  114.5 5.3 %copy.27 = bf16[256,8,2,512]{3,1,2,0:T(8,128)(2,1)} copy(bf16[256,8,2,512]{3,2,1,0:T(2,128)(2,1)} %bitcast.134) | data formatting | bytes 8388608
  119.8 6.6 %copy.25 = bf16[1024,2048]{1,0:T(8,128)(2,1)} copy(bf16[1024,2048]{0,1:T(8,128)(2,1)} %bitcast.125) | data formatting | bytes 8388608 | tf_op jit(solution)/shard_map/dot_general | solution.py:119
  126.4 0.5 collective-permute-start.2
  126.9 6.8 %collective-permute-done = bf16[384,1024]{1,0:T(8,128)(2,1)} collective-permute-done((bf16[384,1024]{1,0:T(8,128)(2,1)}, bf16[384,1024]{1,0:T(8,128)(2,1)}, u32[]{:S(2)}, u32[]{:S(2)}) %collective-permute-start) | collective-permute-done | bytes 786464 | tf_op jit(solution)/shard_map/ppermute | solution.py:38
  133.7 1.5 broadcast_select_fusion.7
  135.1 4.0 %fusion.5 = f32[384,2,512]{2,0,1:T(8,128)S(1)} fusion(bf16[2,512,2048]{2,1,0:T(8,128)(2,1)} %bitcast.135, bf16[384,1024]{1,0:T(8,128)(2,1)S(1)} %get-tuple-element.16, bf16[384,1024]{1,0:T(8,128)(2,1)S(1)} %get-tuple-element.15), kind=kOutput, calls=%fused_computation.15 | convolution fusion | flops 1613758464 | bytes 7340032 | tf_op jit(solution)/shard_map/dot_general | solution.py:119
  139.2 1.0 convolution_convert_fusion.1
  140.2 0.1 broadcast_select_fusion.5
  140.3 1.6 collective-permute-start.1
  141.8 8.6 %collective-permute-done.2 = bf16[384,1024]{1,0:T(8,128)(2,1)S(1)} collective-permute-done((bf16[384,1024]{1,0:T(8,128)(2,1)}, bf16[384,1024]{1,0:T(8,128)(2,1)S(1)}, u32[]{:S(2)}, u32[]{:S(2)}) %collective-permute-start.2) | collective-permute-done | bytes 786464 | tf_op jit(solution)/shard_map/ppermute | solution.py:38
  150.4 0.2 broadcast_select_fusion.4
  150.6 2.1 fusion.30
  152.7 13.8 %collective-permute-done.1 = bf16[384,1024]{1,0:T(8,128)(2,1)S(1)} collective-permute-done((bf16[384,1024]{1,0:T(8,128)(2,1)S(1)}, bf16[384,1024]{1,0:T(8,128)(2,1)S(1)}, u32[]{:S(2)}, u32[]{:S(2)}) %collective-permute-start.1) | collective-permute-done | bytes 786464 | tf_op jit(solution)/shard_map/ppermute | solution.py:52
  166.5 0.4 add_convert_fusion.1
  166.9 1.1 pad_maximum_fusion
  168.0 6.0 %all-to-all-start.1 = ((bf16[16,24,1536]{2,1,0:T(8,128)(2,1)}), bf16[16,24,1536]{2,1,0:T(8,128)(2,1)}, u32[]{:S(2)}, u32[]{:S(2)}) async-start(bf16[16,24,1536]{2,1,0:T(8,128)(2,1)} %bitcast.13), calls=%async_computation.1 | async-start | bytes 2359296 | tf_op jit(solution)/shard_map/all_to_all | solution.py:13
  174.0 0.1 pad_maximum_fusion.2
  174.1 1.2 copy.26
  175.3 4.3 %convolution_convert_fusion = bf16[384,2048]{1,0:T(8,128)(2,1)S(1)} fusion(bf16[384,1024]{0,1:T(8,128)(2,1)} %bitcast.141, bf16[2048,1024]{1,0:T(8,128)(2,1)} %bitcast.126), kind=kOutput, calls=%fused_computation.6 | convolution fusion | flops 1611399168 | bytes 6553600 | tf_op jit(solution)/shard_map/dot_general | solution.py:153
  179.6 0.1 broadcast_select_fusion.2
  179.7 1.6 collective-permute-start.3
  181.2 18.1 %collective-permute-done.3 = bf16[384,1024]{1,0:T(8,128)(2,1)S(1)} collective-permute-done((bf16[384,1024]{1,0:T(8,128)(2,1)S(1)}, bf16[384,1024]{1,0:T(8,128)(2,1)S(1)}, u32[]{:S(2)}, u32[]{:S(2)}) %collective-permute-start.3) | collective-permute-done | bytes 786464 | tf_op jit(solution)/shard_map/ppermute | solution.py:52
  199.3 1.3 add_convert_fusion
  200.6 0.5 all-to-all-done.1
  201.1 5.7 %all-to-all-start.3 = ((bf16[16,24,1024]{2,1,0:T(8,128)(2,1)}), bf16[16,24,1024]{2,1,0:T(8,128)(2,1)S(1)}, u32[]{:S(2)}, u32[]{:S(2)}) async-start(bf16[16,24,1024]{2,1,0:T(8,128)(2,1)} %bitcast.138), calls=%async_computation.3 | async-start | bytes 1572864 | tf_op jit(solution)/shard_map/all_to_all | solution.py:13
  206.8 1.0 slice.65
  207.8 1.1 pad_maximum_fusion.1.block_ref
  208.9 9.8 %reorder.4 = bf16[16,24,1536]{2,1,0:T(8,128)(2,1)} custom-call(s32[16]{0:T(128)} %order_ref.5, bf16[16,24,1536]{2,1,0:T(8,128)(2,1)} %pad_maximum_fusion.1.block_ref), custom_call_target="tpu_custom_call" | custom-call | tf_op jit(solution)/shard_map/reorder/pallas_call | solution.py:22
  218.7 7.0 %all-to-all-done.3 = bf16[16,24,1024]{2,1,0:T(8,128)(2,1)S(1)} async-done(((bf16[16,24,1024]{2,1,0:T(8,128)(2,1)}), bf16[16,24,1024]{2,1,0:T(8,128)(2,1)S(1)}, u32[]{:S(2)}, u32[]{:S(2)}) %all-to-all-start.3) | async-done | bytes 786464 | tf_op jit(solution)/shard_map/all_to_all | solution.py:13
  225.7 5.3 %all-to-all-start.6 = ((bf16[16,24,1536]{2,1,0:T(8,128)(2,1)}), bf16[16,24,1536]{2,1,0:T(8,128)(2,1)S(1)}, u32[]{:S(2)}, u32[]{:S(2)}) async-start(bf16[16,24,1536]{2,1,0:T(8,128)(2,1)} %reorder.4), calls=%async_computation.6 | async-start | bytes 2359296 | tf_op jit(solution)/shard_map/all_to_all | solution.py:13
  231.0 10.1 %reorder.5 = bf16[16,32,2048]{2,1,0:T(8,128)(2,1)} custom-call(s32[16]{0:T(128)} %order_ref.5, bf16[16,32,2048]{2,1,0:T(8,128)(2,1)} %all_to_all.46.block_ref), custom_call_target="tpu_custom_call" | custom-call | tf_op jit(solution)/shard_map/reorder/pallas_call | solution.py:22
  241.1 16.8 %all-to-all-done.6 = bf16[16,24,1536]{2,1,0:T(8,128)(2,1)S(1)} async-done(((bf16[16,24,1536]{2,1,0:T(8,128)(2,1)}), bf16[16,24,1536]{2,1,0:T(8,128)(2,1)S(1)}, u32[]{:S(2)}, u32[]{:S(2)}) %all-to-all-start.6) | async-done | bytes 1179680 | tf_op jit(solution)/shard_map/all_to_all | solution.py:13
  257.9 5.7 %all-to-all-start.8 = ((bf16[16,32,2048]{2,1,0:T(8,128)(2,1)}), bf16[16,32,2048]{2,1,0:T(8,128)(2,1)S(1)}, u32[]{:S(2)}, u32[]{:S(2)}) async-start(bf16[16,32,2048]{2,1,0:T(8,128)(2,1)} %reorder.5), calls=%async_computation.8 | async-start | bytes 4194304 | tf_op jit(solution)/shard_map/all_to_all | solution.py:13
  263.6 10.1 %reorder.3 = bf16[16,32,2048]{2,1,0:T(8,128)(2,1)} custom-call(s32[16]{0:T(128)} %order_ref.5, bf16[16,32,2048]{2,1,0:T(8,128)(2,1)} %all-to-all-done.4.block_ref), custom_call_target="tpu_custom_call" | custom-call | tf_op jit(solution)/shard_map/reorder/pallas_call | solution.py:22
  273.7 35.7 %all-to-all-done.8 = bf16[16,32,2048]{2,1,0:T(8,128)(2,1)S(1)} async-done(((bf16[16,32,2048]{2,1,0:T(8,128)(2,1)}), bf16[16,32,2048]{2,1,0:T(8,128)(2,1)S(1)}, u32[]{:S(2)}, u32[]{:S(2)}) %all-to-all-start.8) | async-done | bytes 2097184 | tf_op jit(solution)/shard_map/all_to_all | solution.py:13
  309.5 6.4 %all-to-all-start.5 = ((bf16[16,32,2048]{2,1,0:T(8,128)(2,1)}), bf16[16,32,2048]{2,1,0:T(8,128)(2,1)}, u32[]{:S(2)}, u32[]{:S(2)}) async-start(bf16[16,32,2048]{2,1,0:T(8,128)(2,1)} %reorder.3), calls=%async_computation.5 | async-start | bytes 4194304 | tf_op jit(solution)/shard_map/all_to_all | solution.py:13
  315.9 2.2 convolution_convert_fusion.3
  318.1 1.2 slice.62
  319.3 0.3 convolution_multiply_fusion.1
  319.6 1.1 fusion.16
  320.7 1.0 slice.67
  321.7 1.5 collective-permute-start.4
  323.2 2.5 convert_multiply_fusion
  325.7 36.1 %all-to-all-done.5 = bf16[16,32,2048]{2,1,0:T(8,128)(2,1)} async-done(((bf16[16,32,2048]{2,1,0:T(8,128)(2,1)}), bf16[16,32,2048]{2,1,0:T(8,128)(2,1)}, u32[]{:S(2)}, u32[]{:S(2)}) %all-to-all-start.5) | async-done | bytes 2097184 | tf_op jit(solution)/shard_map/all_to_all | solution.py:13
  361.8 2.3 convert_multiply_fusion.1
  364.1 1.2 broadcast_select_fusion.1
  365.4 5.6 %convert_bitcast_fusion = (bf16[1,512,2048]{2,1,0:T(8,128)(2,1)}, bf16[1,512,2048]{2,1,0:T(8,128)(2,1)}, bf16[1,512,2048]{2,1,0:T(8,128)(2,1)}) fusion(f32[16,32,2048]{2,1,0:T(8,128)S(1)} %copy-done.2, f32[16,32,2048]{2,1,0:T(8,128)S(1)} %convert_multiply_fusion.1, bf16[384,1024]{1,0:T(8,128)(2,1)S(1)} %get-tuple-element.11, ...), kind=kOutput, calls=%fused_computation.11 | convolution fusion | flops 818937856 | bytes 16646144 | tf_op jit(solution)/shard_map/dot_general | solution.py:164
  (28 shorter events, 0.2 us)
Async XLA Ops:
  0.6 138.5 %copy-start = (bf16[1,512,2048]{2,1,0:T(8,128)(2,1)S(1)}, bf16[1,512,2048]{2,1,0:T(8,128)(2,1)}, u32[]{:S(2)}) copy-start(bf16[1,512,2048]{2,1,0:T(8,128)(2,1)} %param.15) | copy-start | bytes 6291460
  0.6 11.1 %copy-start.7 = (f32[2,64,2]{1,2,0:T(2,128)S(1)}, f32[2,64,2]{1,2,0:T(2,128)}, u32[]{:S(2)}) copy-start(f32[2,64,2]{1,2,0:T(2,128)} %param.12) | copy-start | bytes 3076
  0.7 11.3 %copy-start.6 = (bf16[2,64,1024]{2,1,0:T(8,128)(2,1)S(1)}, bf16[2,64,1024]{2,1,0:T(8,128)(2,1)}, u32[]{:S(2)}) copy-start(bf16[2,64,1024]{2,1,0:T(8,128)(2,1)} %param.10) | copy-start | bytes 786436
  5.4 25.3 %all-to-all-start = ((bf16[16,24,1024]{2,1,0:T(8,128)(2,1)}), bf16[16,24,1024]{2,1,0:T(8,128)(2,1)}, u32[]{:S(2)}, u32[]{:S(2)}) async-start(bf16[16,24,1024]{2,1,0:T(8,128)(2,1)} %bitcast.4), calls=%async_computation | async-start | bytes 1572864 | tf_op jit(solution)/shard_map/all_to_all | solution.py:13
  107.9 60.1 %all-to-all-start.4 = ((bf16[16,32,2048]{2,1,0:T(8,128)(2,1)}), bf16[16,32,2048]{2,1,0:T(8,128)(2,1)}, u32[]{:S(2)}, u32[]{:S(2)}) async-start(bf16[16,32,2048]{2,1,0:T(8,128)(2,1)} %bitcast.140), calls=%async_computation.4 | async-start | bytes 4194304 | tf_op jit(solution)/shard_map/all_to_all | solution.py:13
  113.0 20.7 %collective-permute-start = (bf16[384,1024]{1,0:T(8,128)(2,1)}, bf16[384,1024]{1,0:T(8,128)(2,1)}, u32[]{:S(2)}, u32[]{:S(2)}) collective-permute-start(bf16[384,1024]{1,0:T(8,128)(2,1)} %bitcast.5), channel_id=1, source_target_pairs={{0,16},{16,0},{1,17},{17,1},{2,18},{18,2},{3,19},{19,3},{4,20},{20... | collective-permute-start | bytes 2359304 | tf_op jit(solution)/shard_map/ppermute | solution.py:38
  126.4 24.0 %collective-permute-start.2 = (bf16[384,1024]{1,0:T(8,128)(2,1)}, bf16[384,1024]{1,0:T(8,128)(2,1)S(1)}, u32[]{:S(2)}, u32[]{:S(2)}) collective-permute-start(bf16[384,1024]{1,0:T(8,128)(2,1)} %bitcast.137), channel_id=1, source_target_pairs={{0,16},{16,0},{1,17},{17,1},{2,18},{18,2},{3,19},{19,3},{4,20},{20... | collective-permute-start | bytes 2359304 | tf_op jit(solution)/shard_map/ppermute | solution.py:38
  140.2 10.2 %copy-start.4 = (bf16[16,24,1024]{2,1,0:T(8,128)(2,1)S(1)}, bf16[16,24,1024]{2,1,0:T(8,128)(2,1)}, u32[]{:S(2)}) copy-start(bf16[16,24,1024]{2,1,0:T(8,128)(2,1)} %all_to_all.45) | copy-start | bytes 2359300
  140.3 26.2 %collective-permute-start.1 = (bf16[384,1024]{1,0:T(8,128)(2,1)S(1)}, bf16[384,1024]{1,0:T(8,128)(2,1)S(1)}, u32[]{:S(2)}, u32[]{:S(2)}) collective-permute-start(bf16[384,1024]{1,0:T(8,128)(2,1)S(1)} %broadcast_select_fusion.5), channel_id=1, source_target_pairs={{0,16},{16,0},{1,17},{17,1},{2,18},{18,2},{3,19},{19,3},{4,20},{20... | collective-permute-start | bytes 2359304 | tf_op jit(solution)/shard_map/ppermute | solution.py:52
  166.9 7.1 %copy-start.5 = (bf16[384,1,512]{2,0,1:T(8,128)(2,1)S(1)}, bf16[384,1,512]{2,0,1:T(8,128)(2,1)}, u32[]{:S(2)}) copy-start(bf16[384,1,512]{2,0,1:T(8,128)(2,1)} %get-tuple-element.9) | copy-start | bytes 1179652
  168.0 33.0 %all-to-all-start.1 = ((bf16[16,24,1536]{2,1,0:T(8,128)(2,1)}), bf16[16,24,1536]{2,1,0:T(8,128)(2,1)}, u32[]{:S(2)}, u32[]{:S(2)}) async-start(bf16[16,24,1536]{2,1,0:T(8,128)(2,1)} %bitcast.13), calls=%async_computation.1 | async-start | bytes 2359296 | tf_op jit(solution)/shard_map/all_to_all | solution.py:13
  179.7 19.7 %collective-permute-start.3 = (bf16[384,1024]{1,0:T(8,128)(2,1)S(1)}, bf16[384,1024]{1,0:T(8,128)(2,1)S(1)}, u32[]{:S(2)}, u32[]{:S(2)}) collective-permute-start(bf16[384,1024]{1,0:T(8,128)(2,1)S(1)} %broadcast_select_fusion.2), channel_id=1, source_target_pairs={{0,16},{16,0},{1,17},{17,1},{2,18},{18,2},{3,19},{19,3},{4,20},{20... | collective-permute-start | bytes 2359304 | tf_op jit(solution)/shard_map/ppermute | solution.py:52
  201.1 24.6 %all-to-all-start.3 = ((bf16[16,24,1024]{2,1,0:T(8,128)(2,1)}), bf16[16,24,1024]{2,1,0:T(8,128)(2,1)S(1)}, u32[]{:S(2)}, u32[]{:S(2)}) async-start(bf16[16,24,1024]{2,1,0:T(8,128)(2,1)} %bitcast.138), calls=%async_computation.3 | async-start | bytes 1572864 | tf_op jit(solution)/shard_map/all_to_all | solution.py:13
  225.7 15.4 %copy-start.3 = (bf16[16,24,1024]{2,1,0:T(8,128)(2,1)}, bf16[16,24,1024]{2,1,0:T(8,128)(2,1)S(1)}, u32[]{:S(2)}) copy-start(bf16[16,24,1024]{2,1,0:T(8,128)(2,1)S(1)} %all-to-all-done.3) | copy-start | bytes 2359300
  225.7 32.2 %all-to-all-start.6 = ((bf16[16,24,1536]{2,1,0:T(8,128)(2,1)}), bf16[16,24,1536]{2,1,0:T(8,128)(2,1)S(1)}, u32[]{:S(2)}, u32[]{:S(2)}) async-start(bf16[16,24,1536]{2,1,0:T(8,128)(2,1)} %reorder.4), calls=%async_computation.6 | async-start | bytes 2359296 | tf_op jit(solution)/shard_map/all_to_all | solution.py:13
  257.9 51.6 %all-to-all-start.8 = ((bf16[16,32,2048]{2,1,0:T(8,128)(2,1)}), bf16[16,32,2048]{2,1,0:T(8,128)(2,1)S(1)}, u32[]{:S(2)}, u32[]{:S(2)}) async-start(bf16[16,32,2048]{2,1,0:T(8,128)(2,1)} %reorder.5), calls=%async_computation.8 | async-start | bytes 4194304 | tf_op jit(solution)/shard_map/all_to_all | solution.py:13
  309.5 52.3 %all-to-all-start.5 = ((bf16[16,32,2048]{2,1,0:T(8,128)(2,1)}), bf16[16,32,2048]{2,1,0:T(8,128)(2,1)}, u32[]{:S(2)}, u32[]{:S(2)}) async-start(bf16[16,32,2048]{2,1,0:T(8,128)(2,1)} %reorder.3), calls=%async_computation.5 | async-start | bytes 4194304 | tf_op jit(solution)/shard_map/all_to_all | solution.py:13
  321.7 42.4 %collective-permute-start.4 = (bf16[384,1024]{1,0:T(8,128)(2,1)}, bf16[384,1024]{1,0:T(8,128)(2,1)}, u32[]{:S(2)}, u32[]{:S(2)}) collective-permute-start(bf16[384,1024]{1,0:T(8,128)(2,1)} %slice.67), channel_id=1, source_target_pairs={{0,16},{16,0},{1,17},{17,1},{2,18},{18,2},{3,19},{19,3},{4,20},{20... | collective-permute-start | bytes 2359304 | tf_op jit(solution)/shard_map/ppermute | solution.py:38
  361.8 3.6 copy-start.2
  365.4 5.6 %copy-start.1 = (bf16[1,512,2048]{2,1,0:T(8,128)(2,1)S(1)}, bf16[1,512,2048]{2,1,0:T(8,128)(2,1)}, u32[]{:S(2)}) copy-start(bf16[1,512,2048]{2,1,0:T(8,128)(2,1)} %param.15) | copy-start | bytes 6291460

commit v2 on v1

--- a/solution.py
+++ b/solution.py
@@ -1,3 +1,5 @@
+import functools
+
 import jax
 import jax.numpy as jnp
 from jax import lax
@@ -54,9 +56,178 @@
     return lax.psum_scatter(partial, "dp", scatter_dimension=1, tiled=True)
 
 
-def relocate(array, source, experts):
-    blocks = array.reshape(experts, array.shape[1] // experts, array.shape[2])
-    return exchange(reorder(exchange(blocks), source)).reshape(array.shape[1:])
+def relocate_spread(arrays, source, experts):
+    outputs = []
+    for array in arrays:
+        blocks = array.reshape(experts, array.shape[1] // experts, array.shape[2])
+        outputs.append(exchange(reorder(exchange(blocks), source)).reshape(array.shape[1:]))
+    return outputs
+
+
+PLANES = 4
+GROUP = 4
+KINDS = (((0, 1), (1, 2), (2, 3)), ((0, 2), (2, 3)), ((0, 1), (1, 3)), ((0, 3),))
+KIND_ROW, UP_ROW, DOWN_ROW, FINAL_ROW = 0, 4, 8, 12
+
+
+def plan_kernel(where_ref, source_ref, plan_ref, ends_ref):
+    plane = where_ref[0]
+    member = where_ref[1]
+    for index in range(PLANES):
+        plan_ref[KIND_ROW + index] = 0
+        plan_ref[UP_ROW + index] = GROUP
+        plan_ref[DOWN_ROW + index] = GROUP
+        ends_ref[index] = 0
+    for slot in range(PLANES * GROUP):
+        low = slot // GROUP
+        other = source_ref[slot]
+        high = other // GROUP
+        offset = (slot % GROUP) ^ member
+
+        @pl.when(jnp.logical_and(high == low, plane == low))
+        def _():
+            plan_ref[FINAL_ROW + offset] = (other % GROUP) ^ member
+
+        @pl.when(high > low)
+        def _():
+            turn = jnp.int32(PLANES - 1)
+            for index in reversed(range(PLANES - 1)):
+                turn = jnp.where(ends_ref[index] <= low, index, turn)
+            ends_ref[turn] = high
+            span = high - low
+            kind = jnp.where(span == 3, 4, jnp.where(span == 2, 2 + low, 1))
+            plan_ref[KIND_ROW + turn] = jnp.maximum(plan_ref[KIND_ROW + turn], kind)
+
+            @pl.when(plane == low)
+            def _():
+                plan_ref[UP_ROW + turn] = offset
+                plan_ref[FINAL_ROW + offset] = GROUP + 2 * turn + 1
+
+            @pl.when(plane == high)
+            def _():
+                there = (other % GROUP) ^ member
+                plan_ref[DOWN_ROW + turn] = there
+                plan_ref[FINAL_ROW + there] = GROUP + 2 * turn
+
+
+def make_plan(source, plane, member):
+    smem = pl.BlockSpec(memory_space=pltpu.SMEM)
+    return pl.pallas_call(
+        plan_kernel,
+        out_shape=jax.ShapeDtypeStruct((16,), jnp.int32),
+        in_specs=[smem, smem],
+        out_specs=smem,
+        scratch_shapes=[pltpu.SMEM((PLANES,), jnp.int32)],
+        name="plan",
+    )(jnp.stack([plane, member]), source)
+
+
+def cut_kernel(member_ref, *refs):
+    arrays, outs, sems = refs[:2], refs[2 : 2 + GROUP], refs[-1]
+    rows = outs[0].shape[1]
+    copies = []
+    for offset in range(GROUP):
+        begin = pl.multiple_of((member_ref[0] ^ offset) * rows, rows)
+        for which in range(2):
+            copies.append(
+                pltpu.make_async_copy(
+                    arrays[which].at[pl.ds(begin, rows)],
+                    outs[offset].at[which],
+                    sems.at[offset, which],
+                )
+            )
+    for copy in copies:
+        copy.start()
+    for copy in copies:
+        copy.wait()
+
+
+def cut(first, second, member):
+    rows, width = first.shape
+    anywhere = pl.BlockSpec(memory_space=pl.ANY)
+    piece = jax.ShapeDtypeStruct((2, rows // GROUP, width), first.dtype)
+    return pl.pallas_call(
+        cut_kernel,
+        out_shape=[piece] * GROUP,
+        in_specs=[pl.BlockSpec(memory_space=pltpu.SMEM), anywhere, anywhere],
+        out_specs=[anywhere] * GROUP,
+        scratch_shapes=[pltpu.SemaphoreType.DMA((GROUP, 2))],
+        name="cut",
+    )(member[None], first, second)
+
+
+def choose_kernel(count, choice_ref, *refs):
+    options, outs, sems = refs[:count], refs[count:-1], refs[-1]
+    for place, out in enumerate(outs):
+        for index, option in enumerate(options):
+
+            @pl.when(choice_ref[place] == index)
+            def _():
+                pltpu.make_async_copy(option, out, sems.at[place]).start()
+
+    for place, out in enumerate(outs):
+
+        @pl.when(choice_ref[place] < count)
+        def _():
+            pltpu.make_async_copy(options[0], out, sems.at[place]).wait()
+
+
+def choose(choice, options):
+    anywhere = pl.BlockSpec(memory_space=pl.ANY)
+    piece = jax.ShapeDtypeStruct(options[0].shape, options[0].dtype)
+    return pl.pallas_call(
+        functools.partial(choose_kernel, len(options)),
+        out_shape=[piece] * choice.shape[0],
+        in_specs=[pl.BlockSpec(memory_space=pltpu.SMEM)] + [anywhere] * len(options),
+        out_specs=[anywhere] * choice.shape[0],
+        scratch_shapes=[pltpu.SemaphoreType.DMA((choice.shape[0],))],
+        name="choose",
+    )(choice, *options)
+
+
+def within_plane(offset):
+    return [(index, index ^ offset) for index in range(PLANES * GROUP)]
+
+
+def between_planes(moves):
+    return [(GROUP * a + index, GROUP * b + index) for a, b in moves for index in range(GROUP)]
+
+
+def swap_round(moves):
+    def run(up, down):
+        return (
+            lax.ppermute(up, "expert", between_planes(moves)),
+            lax.ppermute(down, "expert", between_planes([(b, a) for a, b in moves])),
+        )
+
+    return run
+
+
+def relocate_swaps(first, second, source):
+    index = lax.axis_index("expert")
+    plane, member = index // GROUP, index % GROUP
+    plan = make_plan(source, plane, member)
+    pieces = cut(first, second, member)
+    held = [pieces[0]] + [
+        lax.ppermute(pieces[offset], "expert", within_plane(offset)) for offset in range(1, GROUP)
+    ]
+    ways = choose(plan[UP_ROW:FINAL_ROW], held)
+    arrived = []
+    for turn in range(PLANES):
+        arrived += lax.switch(
+            plan[KIND_ROW + turn],
+            [lambda up, down: (up, down)] + [swap_round(moves) for moves in KINDS],
+            ways[turn],
+            ways[PLANES + turn],
+        )
+    ready = choose(plan[FINAL_ROW:], held + arrived)
+    own = [ready[0]] + [
+        lax.ppermute(ready[offset], "expert", within_plane(offset)) for offset in range(1, GROUP)
+    ]
+    for bit in (1, 2):
+        swap = (member & bit) != 0
+        own = [jnp.where(swap, own[offset ^ bit], own[offset]) for offset in range(GROUP)]
+    return [jnp.concatenate([piece[which] for piece in own], axis=0) for which in range(2)]
 
 
 def per_device(
@@ -159,8 +330,10 @@
         plain, back_in.reshape(slots, part_width), preferred_element_type=jnp.float32
     )
 
-    old_first = relocate(moment_first, source, experts)
-    old_second = relocate(moment_second, source, experts)
+    if experts == PLANES * GROUP:
+        old_first, old_second = relocate_swaps(moment_first[0], moment_second[0], source)
+    else:
+        old_first, old_second = relocate_spread((moment_first, moment_second), source, experts)
     down_grad = lax.dot_general(
         there_hidden, there_grads, contract_first, preferred_element_type=jnp.float32
     )

time: 375 us -> 728 us (1.94)
  Pallas kernels: 30.1 us -> 302 us
  starting transfers between devices: 47.1 us -> 163 us
  blocking collectives: 77.2 us -> 33 us
    pallas_call x0 -> x4, Pallas kernels: none -> 292 us  [the longest x2 162 us: choose(): pl.pallas_call(functools.partial(choose_kernel, len(options)), out_shape=...]
    ppermute x0 -> x10, starting transfers between devices: none -> 134 us  [the longest x2 127 us: run(): lax.ppermute(up, 'expert', between_planes(moves))]
    ppermute x0 -> x10, waiting for transfers between devices: none -> 98.4 us  [the longest x3 44.7 us: relocate_swaps(): lax.ppermute(ready[offset], 'expert', within_plane(offset))]
    all_to_all x7 -> x4, waiting for transfers between devices: 114 us -> 23 us  [exchange(): lax.all_to_all(blocks, 'expert', split_axis=0, concat_axis=0, tiled=True)]
    all_to_all x2 -> x1, blocking collectives: 77.2 us -> 33 us  [exchange(): lax.all_to_all(blocks, 'expert', split_axis=0, concat_axis=0, tiled=True)]
    pallas_call x3 -> x1, Pallas kernels: 30.1 us -> 9.84 us  [reorder(): pl.pallas_call(copy_block, out_shape=jax.ShapeDtypeStruct(blocks.shape, b...]
    ppermute x2, waiting for transfers between devices: 31.9 us -> 13.1 us  [scatter_sum(): other = lax.ppermute(send, 'dp', ((0, 1), (1, 0)))]
    all_to_all x7 -> x4, starting transfers between devices: 40.4 us -> 21.8 us  [exchange(): lax.all_to_all(blocks, 'expert', split_axis=0, concat_axis=0, tiled=True)]
  transfers between devices with their start and end apart: 12 -> 19, of which waited for: 10 -> 11; matrix products, arithmetic and copies ran while one was open for 11% -> 7% of each run, Pallas kernels for 8% -> 40%
where the time goes in v2:
time: 728 us; the launch traced here: 725 us
  Pallas kernels  302 us (41%)
  starting transfers between devices  163 us (22%)
  waiting for transfers between devices  160 us (22%)
  blocking collectives  33 us (5%)
  local copies, waits for them, and re-layouts  24.4 us (3%)
  matrix products  24.3 us (3%)
  other arithmetic  14.7 us (2%)
    pallas_call x2, Pallas kernels, choose(): pl.pallas_call(functools.partial(choose_kernel, len(options)), out_shape=...  162 us
    pallas_call x1, Pallas kernels, cut(): pl.pallas_call(cut_kernel, out_shape=[piece] * GROUP, in_specs=[pl.BlockS...  128 us
    ppermute x2, starting transfers between devices, run(): lax.ppermute(up, 'expert', between_planes(moves))  127 us
    ppermute x3, waiting for transfers between devices, relocate_swaps(): lax.ppermute(ready[offset], 'expert', within_plane(offset))  44.7 us
    all_to_all x1, blocking collectives, exchange(): lax.all_to_all(blocks, 'expert', split_axis=0, concat_axis=0, tiled=True)  33 us
    ppermute x3, waiting for transfers between devices, relocate_swaps(): lax.ppermute(pieces[offset], 'expert', within_plane(offset))  31.6 us
    ppermute x3, waiting for transfers between devices, gather_features(): other = lax.ppermute(rows, 'dp', ((0, 1), (1, 0)))  25.1 us
    all_to_all x4, waiting for transfers between devices, exchange(): lax.all_to_all(blocks, 'expert', split_axis=0, concat_axis=0, tiled=True)  23 us
  transfers between devices with their start and end apart: 19, of which 11 were waited for; matrix products, arithmetic and copies ran while one was open for 7% of the time, Pallas kernels for 40%

profile of v2, /device:TPU:8, one launch (start us, length us, event | category | flops | bytes accessed | tf_op | source)
XLA Modules:
  0.0 724.7 jit_solution(5797028763695066584)
XLA Ops:
  0.7 0.9 copy.23
  1.6 0.7 broadcast_multiply_fusion
  3.1 2.3 convolution_convert_fusion.2
  5.4 6.3 all-to-all-start
  12.0 1.4 multiply_convert_fusion
  13.4 17.3 %all-to-all-done = bf16[16,24,1024]{2,1,0:T(8,128)(2,1)S(1)} async-done(((bf16[16,24,1024]{2,1,0:T(8,128)(2,1)}), bf16[16,24,1024]{2,1,0:T(8,128)(2,1)S(1)}, u32[]{:S(2)}, u32[]{:S(2)}) %all-to-all-start) | async-done | bytes 786464 | tf_op jit(solution)/shard_map/all_to_all | solution.py:15
  30.7 5.3 all-to-all-start.2
  35.9 1.5 collective-permute-start.32
  37.4 5.4 copy.27
  42.8 6.5 copy.25
  49.3 5.7 all-to-all-done.2
  55.0 1.5 collective-permute-start.34
  56.5 1.2 broadcast_select_fusion.15
  57.7 4.0 fusion.9
  61.7 1.0 convolution_convert_fusion.1
  62.8 0.7 collective-permute-start.33
  63.6 12.0 %collective-permute-done.34 = bf16[384,1024]{1,0:T(8,128)(2,1)S(1)} collective-permute-done((bf16[384,1024]{1,0:T(8,128)(2,1)}, bf16[384,1024]{1,0:T(8,128)(2,1)S(1)}, u32[]{:S(2)}, u32[]{:S(2)}) %collective-permute-start.34) | collective-permute-done | bytes 786464 | tf_op jit(solution)/shard_map/ppermute | solution.py:40
  75.6 1.2 broadcast_select_fusion.12
  76.8 2.3 fusion.34
  79.1 13.1 %collective-permute-done.33 = bf16[384,1024]{1,0:T(8,128)(2,1)S(1)} collective-permute-done((bf16[384,1024]{1,0:T(8,128)(2,1)S(1)}, bf16[384,1024]{1,0:T(8,128)(2,1)S(1)}, u32[]{:S(2)}, u32[]{:S(2)}) %collective-permute-start.33) | collective-permute-done | bytes 786464 | tf_op jit(solution)/shard_map/ppermute | solution.py:54
  92.8 33.0 %all_to_all.25 = bf16[16,24,1536]{2,1,0:T(8,128)(2,1)S(1)} all-to-all(bf16[16,24,1536]{2,1,0:T(8,128)(2,1)S(1)} %bitcast.142), channel_id=1, replica_groups=mesh['dp'=2,'expert'=16] {'expert'}, dimensions={0} | all-to-all | bytes 2359296 | tf_op jit(solution)/shard_map/all_to_all | solution.py:15
  125.8 2.6 pad_maximum_fusion.3.block_ref
  128.4 9.8 %reorder.1 = bf16[16,24,1536]{2,1,0:T(8,128)(2,1)} custom-call(s32[16]{0:T(128)} %order_ref.1, bf16[16,24,1536]{2,1,0:T(8,128)(2,1)} %pad_maximum_fusion.3.block_ref), custom_call_target="tpu_custom_call" | custom-call | tf_op jit(solution)/shard_map/reorder/pallas_call | solution.py:24
  138.3 4.7 all-to-all-start.4
  143.0 128.2 %cut.1 = (bf16[2,128,2048]{2,1,0:T(8,128)(2,1)}, bf16[2,128,2048]{2,1,0:T(8,128)(2,1)}, bf16[2,128,2048]{2,1,0:T(8,128)(2,1)}, bf16[2,128,2048]{2,1,0:T(8,128)(2,1)}) custom-call(s32[1]{0:T(128)} %bitcast.27.member_ref, bf16[512,2048]{1,0:T(8,128)(2,1)} %bitcast.147, bf16[512,2048]{1,0:T(8,128)(2,1)} %bitcast.148), custom_call_target="tpu_custom_call" | custom-call | tf_op jit(solution)/shard_map/cut/pallas_call | solution.py:149
  271.4 1.5 collective-permute-start.37
  273.1 0.7 pad_add_fusion.where_ref
  273.8 1.5 plan.1
  275.4 1.2 copy.26
  276.5 4.3 convolution_convert_fusion
  280.8 1.0 broadcast_select_fusion.10
  281.8 1.5 collective-permute-start.35
  283.3 0.6 fusion.53
  287.4 10.3 %collective-permute-done.37.refs_2_ = bf16[2,128,2048]{2,1,0:T(8,128)(2,1)} collective-permute-done((bf16[2,128,2048]{2,1,0:T(8,128)(2,1)}, bf16[2,128,2048]{2,1,0:T(8,128)(2,1)}, u32[]{:S(2)}, u32[]{:S(2)}) %collective-permute-start.37) | collective-permute-done | bytes 1048608 | tf_op jit(solution)/shard_map/ppermute | solution.py:212
  297.7 21.3 %collective-permute-done.38.refs_3_ = bf16[2,128,2048]{2,1,0:T(8,128)(2,1)} collective-permute-done((bf16[2,128,2048]{2,1,0:T(8,128)(2,1)}, bf16[2,128,2048]{2,1,0:T(8,128)(2,1)}, u32[]{:S(2)}, u32[]{:S(2)}) %collective-permute-start.38) | collective-permute-done | bytes 1048608 | tf_op jit(solution)/shard_map/ppermute | solution.py:212
  319.1 33.6 %choose.2 = (bf16[2,128,2048]{2,1,0:T(8,128)(2,1)}, bf16[2,128,2048]{2,1,0:T(8,128)(2,1)}, bf16[2,128,2048]{2,1,0:T(8,128)(2,1)}, bf16[2,128,2048]{2,1,0:T(8,128...) custom-call(s32[8]{0:T(128)} %slice.99.choice_ref, ...), custom_call_target="tpu_custom_call" | custom-call | tf_op jit(solution)/shard_map/choose/pallas_call | solution.py:178
  352.7 3.7 conditional.4
  352.9 0.7 collective-permute-start.2
  353.6 0.7 collective-permute-start.3
  354.4 1.0 copy.32
  355.4 1.0 copy.33
  356.4 153.3 %conditional.5 = ((bf16[2,128,2048]{2,1,0:T(8,128)(2,1)}, bf16[2,128,2048]{2,1,0:T(8,128)(2,1)})) conditional(s32[]{:T(128)} %bitcast.31, (bf16[2,128,2048]{2,1,0:T(8,128)(2,1)}, bf16[2,128,2048]{2,1,0:T(8,128)(2,1)}) %tuple.85, (bf16[2,128,2048]{2,1,0:T(8,128)(2,1)}, bf16[2,128,2048]{2,1,0:T(8,128)(2,1)}) %tuple.85, ...), branch_computations={%region_8.9_spmd, %region_9.10_spmd, %region_10.11_spmd, %region_1... | conditional | bytes 12583016 | solution.py:217
  356.4 126.0 %collective-permute-start.8 = (bf16[2,128,2048]{2,1,0:T(8,128)(2,1)}, bf16[2,128,2048]{2,1,0:T(8,128)(2,1)S(1)}, u32[]{:S(2)}, u32[]{:S(2)}) collective-permute-start(bf16[2,128,2048]{2,1,0:T(8,128)(2,1)} %get-tuple-element.88), channel_id=1, source_target_pairs={{0,4},{1,5},{2,6},{3,7},{4,8},{5,9},{6,10},{7,11},{8,12},{9,13},{1... | collective-permute-start | bytes 3145736 | tf_op jit(solution)/shard_map/cond/branch_1_fun/ppermute | solution.py:199
  482.4 3.2 collective-permute-start.9
  485.6 20.8 %collective-permute-done.8 = bf16[2,128,2048]{2,1,0:T(8,128)(2,1)S(1)} collective-permute-done((bf16[2,128,2048]{2,1,0:T(8,128)(2,1)}, bf16[2,128,2048]{2,1,0:T(8,128)(2,1)S(1)}, u32[]{:S(2)}, u32[]{:S(2)}) %collective-permute-start.8) | collective-permute-done | bytes 1048608 | tf_op jit(solution)/shard_map/cond/branch_1_fun/ppermute | solution.py:199
  506.4 1.0 copy.40
  507.4 1.2 collective-permute-done.9
  508.6 1.0 copy.41
  509.7 128.9 %choose.3 = (bf16[2,128,2048]{2,1,0:T(8,128)(2,1)}, bf16[2,128,2048]{2,1,0:T(8,128)(2,1)}, bf16[2,128,2048]{2,1,0:T(8,128)(2,1)}, bf16[2,128,2048]{2,1,0:T(8,128)(2,1)}) custom-call(s32[4]{0:T(128)} %slice.97.choice_ref, bf16[2,128,2048]{2,1,0:T(8,128)(2,1)} %get-tuple-element.141.refs_0_, bf16[2,128,2048]{2,1,0:T(8,128)(2,1)} %collective-permute-done.36.refs_1_, ...), custom_call_target="tpu_custom_call" | custom-call | tf_op jit(solution)/shard_map/choose/pallas_call | solution.py:178
  638.6 1.6 collective-permute-start.40
  640.5 2.4 add_convert_fusion
  642.9 5.6 all-to-all-start.3
  648.5 22.2 %collective-permute-done.39 = bf16[2,128,2048]{2,1,0:T(8,128)(2,1)} collective-permute-done((bf16[2,128,2048]{2,1,0:T(8,128)(2,1)}, bf16[2,128,2048]{2,1,0:T(8,128)(2,1)}, u32[]{:S(2)}, u32[]{:S(2)}) %collective-permute-start.39) | collective-permute-done | bytes 1048608 | tf_op jit(solution)/shard_map/ppermute | solution.py:225
  670.6 22.6 %collective-permute-done.40 = bf16[2,128,2048]{2,1,0:T(8,128)(2,1)} collective-permute-done((bf16[2,128,2048]{2,1,0:T(8,128)(2,1)}, bf16[2,128,2048]{2,1,0:T(8,128)(2,1)}, u32[]{:S(2)}, u32[]{:S(2)}) %collective-permute-start.40) | collective-permute-done | bytes 1048608 | tf_op jit(solution)/shard_map/ppermute | solution.py:225
  693.2 2.5 broadcast_select_fusion.7
  695.7 1.4 slice_bitcast_fusion.4
  697.1 1.0 slice.127
  698.1 1.5 collective-permute-start.42
  699.6 1.4 slice_bitcast_fusion.6
  701.0 2.2 convolution_convert_fusion.3
  703.8 1.1 fusion.20
  704.8 13.1 %collective-permute-done.42 = bf16[384,1024]{1,0:T(8,128)(2,1)} collective-permute-done((bf16[384,1024]{1,0:T(8,128)(2,1)}, bf16[384,1024]{1,0:T(8,128)(2,1)}, u32[]{:S(2)}, u32[]{:S(2)}) %collective-permute-start.42) | collective-permute-done | bytes 786464 | tf_op jit(solution)/shard_map/ppermute | solution.py:40
  717.9 1.2 broadcast_select_fusion.9
  719.2 5.5 fusion.3
  (74 shorter events, 4.2 us)
Async XLA Ops:
  0.6 61.1 %copy-start = (bf16[1,512,2048]{2,1,0:T(8,128)(2,1)S(1)}, bf16[1,512,2048]{2,1,0:T(8,128)(2,1)}, u32[]{:S(2)}) copy-start(bf16[1,512,2048]{2,1,0:T(8,128)(2,1)} %param.35) | copy-start | bytes 6291460
  0.6 11.1 %copy-start.16 = (f32[2,64,2]{1,2,0:T(2,128)S(1)}, f32[2,64,2]{1,2,0:T(2,128)}, u32[]{:S(2)}) copy-start(f32[2,64,2]{1,2,0:T(2,128)} %param.32) | copy-start | bytes 3076
  0.7 11.3 %copy-start.14 = (bf16[2,64,1024]{2,1,0:T(8,128)(2,1)S(1)}, bf16[2,64,1024]{2,1,0:T(8,128)(2,1)}, u32[]{:S(2)}) copy-start(bf16[2,64,1024]{2,1,0:T(8,128)(2,1)} %param.30) | copy-start | bytes 786436
  5.4 25.2 %all-to-all-start = ((bf16[16,24,1024]{2,1,0:T(8,128)(2,1)}), bf16[16,24,1024]{2,1,0:T(8,128)(2,1)S(1)}, u32[]{:S(2)}, u32[]{:S(2)}) async-start(bf16[16,24,1024]{2,1,0:T(8,128)(2,1)} %bitcast.4), calls=%async_computation | async-start | bytes 1572864 | tf_op jit(solution)/shard_map/all_to_all | solution.py:15
  30.7 24.3 %all-to-all-start.2 = ((bf16[16,24,1024]{2,1,0:T(8,128)(2,1)}), bf16[16,24,1024]{2,1,0:T(8,128)(2,1)}, u32[]{:S(2)}, u32[]{:S(2)}) async-start(bf16[16,24,1024]{2,1,0:T(8,128)(2,1)} %bitcast.18), calls=%async_computation.2 | async-start | bytes 1572864 | tf_op jit(solution)/shard_map/all_to_all | solution.py:15
  35.9 20.5 %collective-permute-start.32 = (bf16[384,1024]{1,0:T(8,128)(2,1)S(1)}, bf16[384,1024]{1,0:T(8,128)(2,1)}, u32[]{:S(2)}, u32[]{:S(2)}) collective-permute-start(bf16[384,1024]{1,0:T(8,128)(2,1)S(1)} %bitcast.145), channel_id=1, source_target_pairs={{0,16},{16,0},{1,17},{17,1},{2,18},{18,2},{3,19},{19,3},{4,20},{20... | collective-permute-start | bytes 2359304 | tf_op jit(solution)/shard_map/ppermute | solution.py:40
  55.0 20.6 %collective-permute-start.34 = (bf16[384,1024]{1,0:T(8,128)(2,1)}, bf16[384,1024]{1,0:T(8,128)(2,1)S(1)}, u32[]{:S(2)}, u32[]{:S(2)}) collective-permute-start(bf16[384,1024]{1,0:T(8,128)(2,1)} %bitcast.19), channel_id=1, source_target_pairs={{0,16},{16,0},{1,17},{17,1},{2,18},{18,2},{3,19},{19,3},{4,20},{20... | collective-permute-start | bytes 2359304 | tf_op jit(solution)/shard_map/ppermute | solution.py:40
  62.8 29.4 %collective-permute-start.33 = (bf16[384,1024]{1,0:T(8,128)(2,1)S(1)}, bf16[384,1024]{1,0:T(8,128)(2,1)S(1)}, u32[]{:S(2)}, u32[]{:S(2)}) collective-permute-start(bf16[384,1024]{1,0:T(8,128)(2,1)S(1)} %broadcast_select_fusion.13), channel_id=1, source_target_pairs={{0,16},{16,0},{1,17},{17,1},{2,18},{18,2},{3,19},{19,3},{4,20},{20... | collective-permute-start | bytes 2359304 | tf_op jit(solution)/shard_map/ppermute | solution.py:54
  125.8 12.5 %copy-start.2 = (bf16[16,24,1536]{2,1,0:T(8,128)(2,1)}, bf16[16,24,1536]{2,1,0:T(8,128)(2,1)S(1)}, u32[]{:S(2)}) copy-start(bf16[16,24,1536]{2,1,0:T(8,128)(2,1)S(1)} %all_to_all.25) | copy-start | bytes 3538948
  138.3 504.6 %all-to-all-start.4 = ((bf16[16,24,1536]{2,1,0:T(8,128)(2,1)}), bf16[16,24,1536]{2,1,0:T(8,128)(2,1)S(1)}, u32[]{:S(2)}, u32[]{:S(2)}) async-start(bf16[16,24,1536]{2,1,0:T(8,128)(2,1)} %reorder.1), calls=%async_computation.4 | async-start | bytes 2359296 | tf_op jit(solution)/shard_map/all_to_all | solution.py:15
  142.9 132.3 %copy-start.12 = (bf16[384,1,512]{2,0,1:T(8,128)(2,1)S(1)}, bf16[384,1,512]{2,0,1:T(8,128)(2,1)}, u32[]{:S(2)}) copy-start(bf16[384,1,512]{2,0,1:T(8,128)(2,1)} %get-tuple-element.172) | copy-start | bytes 1179652
  142.9 132.3 %copy-start.13 = (bf16[384,1,512]{2,0,1:T(8,128)(2,1)S(1)}, bf16[384,1,512]{2,0,1:T(8,128)(2,1)}, u32[]{:S(2)}) copy-start(bf16[384,1,512]{2,0,1:T(8,128)(2,1)} %get-tuple-element.173) | copy-start | bytes 1179652
  271.2 16.2 %collective-permute-start.36 = (bf16[2,128,2048]{2,1,0:T(8,128)(2,1)}, bf16[2,128,2048]{2,1,0:T(8,128)(2,1)}, u32[]{:S(2)}, u32[]{:S(2)}) collective-permute-start(bf16[2,128,2048]{2,1,0:T(8,128)(2,1)} %get-tuple-element.142), channel_id=1, source_target_pairs={{0,1},{1,0},{2,3},{3,2},{4,5},{5,4},{6,7},{7,6},{8,9},{9,8},{10,11... | collective-permute-start | bytes 3145736 | tf_op jit(solution)/shard_map/ppermute | solution.py:212
  271.4 26.3 %collective-permute-start.37 = (bf16[2,128,2048]{2,1,0:T(8,128)(2,1)}, bf16[2,128,2048]{2,1,0:T(8,128)(2,1)}, u32[]{:S(2)}, u32[]{:S(2)}) collective-permute-start(bf16[2,128,2048]{2,1,0:T(8,128)(2,1)} %get-tuple-element.143), channel_id=1, source_target_pairs={{0,2},{1,3},{2,0},{3,1},{4,6},{5,7},{6,4},{7,5},{8,10},{9,11},{10,... | collective-permute-start | bytes 3145736 | tf_op jit(solution)/shard_map/ppermute | solution.py:212
  272.9 46.1 %collective-permute-start.38 = (bf16[2,128,2048]{2,1,0:T(8,128)(2,1)}, bf16[2,128,2048]{2,1,0:T(8,128)(2,1)}, u32[]{:S(2)}, u32[]{:S(2)}) collective-permute-start(bf16[2,128,2048]{2,1,0:T(8,128)(2,1)} %get-tuple-element.144), channel_id=1, source_target_pairs={{0,3},{1,2},{2,1},{3,0},{4,7},{5,6},{6,5},{7,4},{8,11},{9,10},{10,... | collective-permute-start | bytes 3145736 | tf_op jit(solution)/shard_map/ppermute | solution.py:212
  280.8 2.5 copy-start.15
  281.8 358.6 %collective-permute-start.35 = (bf16[384,1024]{1,0:T(8,128)(2,1)}, bf16[384,1024]{1,0:T(8,128)(2,1)}, u32[]{:S(2)}, u32[]{:S(2)}) collective-permute-start(bf16[384,1024]{1,0:T(8,128)(2,1)} %broadcast_select_fusion.10), channel_id=1, source_target_pairs={{0,16},{16,0},{1,17},{17,1},{2,18},{18,2},{3,19},{19,3},{4,20},{20... | collective-permute-start | bytes 2359304 | tf_op jit(solution)/shard_map/ppermute | solution.py:54
  352.9 1.5 collective-permute-start.2
  353.6 1.7 collective-permute-start.3
  356.4 150.1 %collective-permute-start.8 = (bf16[2,128,2048]{2,1,0:T(8,128)(2,1)}, bf16[2,128,2048]{2,1,0:T(8,128)(2,1)S(1)}, u32[]{:S(2)}, u32[]{:S(2)}) collective-permute-start(bf16[2,128,2048]{2,1,0:T(8,128)(2,1)} %get-tuple-element.88), channel_id=1, source_target_pairs={{0,4},{1,5},{2,6},{3,7},{4,8},{5,9},{6,10},{7,11},{8,12},{9,13},{1... | collective-permute-start | bytes 3145736 | tf_op jit(solution)/shard_map/cond/branch_1_fun/ppermute | solution.py:199
  482.4 26.2 %collective-permute-start.9 = (bf16[2,128,2048]{2,1,0:T(8,128)(2,1)}, bf16[2,128,2048]{2,1,0:T(8,128)(2,1)S(1)}, u32[]{:S(2)}, u32[]{:S(2)}) collective-permute-start(bf16[2,128,2048]{2,1,0:T(8,128)(2,1)} %get-tuple-element.89), channel_id=1, source_target_pairs={{4,0},{5,1},{6,2},{7,3},{8,4},{9,5},{10,6},{11,7},{12,8},{13,9},{1... | collective-permute-start | bytes 3145736 | tf_op jit(solution)/shard_map/cond/branch_1_fun/ppermute | solution.py:200
  638.5 32.1 %collective-permute-start.39 = (bf16[2,128,2048]{2,1,0:T(8,128)(2,1)}, bf16[2,128,2048]{2,1,0:T(8,128)(2,1)}, u32[]{:S(2)}, u32[]{:S(2)}) collective-permute-start(bf16[2,128,2048]{2,1,0:T(8,128)(2,1)} %get-tuple-element.161), channel_id=1, source_target_pairs={{0,3},{1,2},{2,1},{3,0},{4,7},{5,6},{6,5},{7,4},{8,11},{9,10},{10,... | collective-permute-start | bytes 3145736 | tf_op jit(solution)/shard_map/ppermute | solution.py:225
  638.6 54.6 %collective-permute-start.40 = (bf16[2,128,2048]{2,1,0:T(8,128)(2,1)}, bf16[2,128,2048]{2,1,0:T(8,128)(2,1)}, u32[]{:S(2)}, u32[]{:S(2)}) collective-permute-start(bf16[2,128,2048]{2,1,0:T(8,128)(2,1)} %get-tuple-element.162), channel_id=1, source_target_pairs={{0,2},{1,3},{2,0},{3,1},{4,6},{5,7},{6,4},{7,5},{8,10},{9,11},{10,... | collective-permute-start | bytes 3145736 | tf_op jit(solution)/shard_map/ppermute | solution.py:225
  640.2 53.0 %collective-permute-start.41 = (bf16[2,128,2048]{2,1,0:T(8,128)(2,1)}, bf16[2,128,2048]{2,1,0:T(8,128)(2,1)}, u32[]{:S(2)}, u32[]{:S(2)}) collective-permute-start(bf16[2,128,2048]{2,1,0:T(8,128)(2,1)} %get-tuple-element.163), channel_id=1, source_target_pairs={{0,1},{1,0},{2,3},{3,2},{4,5},{5,4},{6,7},{7,6},{8,9},{9,8},{10,11... | collective-permute-start | bytes 3145736 | tf_op jit(solution)/shard_map/ppermute | solution.py:225
  642.9 58.1 %all-to-all-start.3 = ((bf16[16,24,1024]{2,1,0:T(8,128)(2,1)}), bf16[16,24,1024]{2,1,0:T(8,128)(2,1)}, u32[]{:S(2)}, u32[]{:S(2)}) async-start(bf16[16,24,1024]{2,1,0:T(8,128)(2,1)} %bitcast.146), calls=%async_computation.3 | async-start | bytes 1572864 | tf_op jit(solution)/shard_map/all_to_all | solution.py:15
  698.1 19.8 %collective-permute-start.42 = (bf16[384,1024]{1,0:T(8,128)(2,1)}, bf16[384,1024]{1,0:T(8,128)(2,1)}, u32[]{:S(2)}, u32[]{:S(2)}) collective-permute-start(bf16[384,1024]{1,0:T(8,128)(2,1)} %slice.127), channel_id=1, source_target_pairs={{0,16},{16,0},{1,17},{17,1},{2,18},{18,2},{3,19},{19,3},{4,20},{20... | collective-permute-start | bytes 2359304 | tf_op jit(solution)/shard_map/ppermute | solution.py:40
  699.6 3.6 copy-start.3
  703.7 15.5 %copy-start.4 = (bf16[128,2048]{1,0:T(8,128)(2,1)S(1)}, bf16[128,2048]{1,0:T(8,128)(2,1)}, u32[]{:S(2)}) copy-start(bf16[128,2048]{1,0:T(8,128)(2,1)} %get-tuple-element.187) | copy-start | bytes 1572868
  703.7 15.5 %copy-start.5 = (bf16[128,2048]{1,0:T(8,128)(2,1)S(1)}, bf16[128,2048]{1,0:T(8,128)(2,1)}, u32[]{:S(2)}) copy-start(bf16[128,2048]{1,0:T(8,128)(2,1)} %get-tuple-element.188) | copy-start | bytes 1572868
  703.7 15.5 %copy-start.6 = (bf16[128,2048]{1,0:T(8,128)(2,1)S(1)}, bf16[128,2048]{1,0:T(8,128)(2,1)}, u32[]{:S(2)}) copy-start(bf16[128,2048]{1,0:T(8,128)(2,1)} %get-tuple-element.199) | copy-start | bytes 1572868
  703.7 15.5 %copy-start.7 = (bf16[128,2048]{1,0:T(8,128)(2,1)S(1)}, bf16[128,2048]{1,0:T(8,128)(2,1)}, u32[]{:S(2)}) copy-start(bf16[128,2048]{1,0:T(8,128)(2,1)} %get-tuple-element.200) | copy-start | bytes 1572868
  703.7 15.5 %copy-start.8 = (bf16[128,2048]{1,0:T(8,128)(2,1)S(1)}, bf16[128,2048]{1,0:T(8,128)(2,1)}, u32[]{:S(2)}) copy-start(bf16[128,2048]{1,0:T(8,128)(2,1)} %get-tuple-element.183) | copy-start | bytes 1572868
  703.7 15.5 %copy-start.9 = (bf16[128,2048]{1,0:T(8,128)(2,1)S(1)}, bf16[128,2048]{1,0:T(8,128)(2,1)}, u32[]{:S(2)}) copy-start(bf16[128,2048]{1,0:T(8,128)(2,1)} %get-tuple-element.184) | copy-start | bytes 1572868
  703.7 15.5 %copy-start.10 = (bf16[128,2048]{1,0:T(8,128)(2,1)S(1)}, bf16[128,2048]{1,0:T(8,128)(2,1)}, u32[]{:S(2)}) copy-start(bf16[128,2048]{1,0:T(8,128)(2,1)} %get-tuple-element.201) | copy-start | bytes 1572868
  703.7 15.5 %copy-start.11 = (bf16[128,2048]{1,0:T(8,128)(2,1)S(1)}, bf16[128,2048]{1,0:T(8,128)(2,1)}, u32[]{:S(2)}) copy-start(bf16[128,2048]{1,0:T(8,128)(2,1)} %get-tuple-element.202) | copy-start | bytes 1572868
  719.2 5.5 copy-start.1
